TPU v7x, 32 devices: a whole 2x2x4 slice. The times are simulated.
32 devices in a mesh: seq: 4 (over y, x), batch: 8 (over z, core).
Axes of the slice: x: 2, y: 2, z: 4, core: 2. Of those that a mesh axis runs over, the one named last changes fastest.
Arguments:
- inputs: bfloat16 [8, 2048, 768], P('batch', 'seq'), may hold values from -6 to 6
- doc_ids: int32 [8, 2048], P('batch'), may hold values from 0 to 6, as said below
- w_qkv: bfloat16 [768, 896], replicated, may hold values from -0.3125 to 0.3125
- b_qkv: float32 [896], replicated, may hold values from -3 to 3
- w_o: bfloat16 [768, 768], replicated, may hold values from -0.875 to 0.875
- w_fc: bfloat16 [768, 3072], replicated, may hold values from -0.21875 to 0.21875
- b_fc: float32 [3072], replicated, may hold values from -3 to 3
- w_proj: bfloat16 [3072, 768], replicated, may hold values from -0.109375 to 0.109375
- b_proj: float32 [768], replicated, may hold values from -3 to 3
- gain_one: float32 [768], replicated, may hold values from 0.1 to 1.9
- shift_one: float32 [768], replicated, may hold values from -1.75 to 1.75
- gain_two: float32 [768], replicated, may hold values from 0.1 to 1.9
- shift_two: float32 [768], replicated, may hold values from -1.75 to 1.75
- cotangent: bfloat16 [8, 2048, 768], P('batch', 'seq'), may hold values from -6 to 6
Outputs:
- outputs: bfloat16 [8, 2048, 768], P('batch', 'seq')
- input_grads: bfloat16 [8, 2048, 768], P('batch', 'seq')
- grad_w_qkv: float32 [768, 896], P('batch')
- grad_b_qkv: float32 [896], P('batch')
- grad_w_o: float32 [768, 768], P('batch')
- grad_w_fc: float32 [768, 3072], P('batch')
- grad_b_fc: float32 [3072], P('batch')
- grad_w_proj: float32 [3072, 768], P('batch')
- grad_b_proj: float32 [768], P('batch')
- grad_gain_one: float32 [768], P('batch')
- grad_shift_one: float32 [768], P('batch')
- grad_gain_two: float32 [768], P('batch')
- grad_shift_two: float32 [768], P('batch')
Inputs may be any that keep to these rules, and one draw needn't show every extreme that they name: `doc_ids`: along each row the ids never fall; in every row one document begins within the first 512 positions and ends within the last 512.
All inputs are finite; a program needn't handle non-finite values.
Results may differ from a plain program's by a relative error of at most 0.017.
Values may be sent and summed in bfloat16 or wider, within the bound.
A program may use at most 320 MiB of HBM per device.

v0:
```python
from functools import partial
import math

import jax
import jax.numpy as jnp
from jax import lax
from jax.sharding import PartitionSpec as P

HEAD = 64
ROT = 16


EPSILON = 1e-05


def from_behind(block, axis, distance):
    devices = range(lax.axis_size(axis))
    route = [(i - distance, i) for i in devices if i - distance in devices]
    return lax.ppermute(block, axis, route)


def norm_parts(tokens):
    average = jnp.mean(tokens, axis=-1, keepdims=True)
    centered = tokens - average
    variance = jnp.mean(centered * centered, axis=-1, keepdims=True)
    inverse_std = lax.rsqrt(variance + EPSILON)
    return (centered * inverse_std, inverse_std)


def norm_back(scaled, normed, inverse_std):
    first = jnp.mean(scaled, axis=-1, keepdims=True)
    second = jnp.mean(scaled * normed, axis=-1, keepdims=True)
    return inverse_std * (scaled - first - normed * second)


def rotate(values, cosine, sine):
    half = ROT // 2
    first = values[..., :half]
    second = values[..., half:ROT]
    return jnp.concatenate(
        [first * cosine - second * sine, second * cosine + first * sine, values[..., ROT:]], axis=-1
    )


def rotate_back(grads, cosine, sine):
    half = ROT // 2
    first = grads[..., :half]
    second = grads[..., half:ROT]
    return jnp.concatenate(
        [first * cosine + second * sine, second * cosine - first * sine, grads[..., ROT:]], axis=-1
    )


def per_device(
    inputs,
    doc_ids,
    w_qkv,
    b_qkv,
    w_o,
    w_fc,
    b_fc,
    w_proj,
    b_proj,
    gain_one,
    shift_one,
    gain_two,
    shift_two,
    cotangent,
):
    rows_here, span, width = inputs.shape
    count = rows_here * span
    heads = width // HEAD
    parts = lax.axis_size("seq")
    mine = lax.axis_index("seq")
    scale = 1.0 / math.sqrt(HEAD)
    tokens = inputs.reshape(count, width).astype(jnp.float32)
    normed, inverse_std = norm_parts(tokens)
    first_in = (normed * gain_one + shift_one).astype(jnp.bfloat16)
    second_in = (normed * gain_two + shift_two).astype(jnp.bfloat16)
    project = jnp.dot(first_in, w_qkv, preferred_element_type=jnp.float32) + b_qkv
    project = project.reshape(rows_here, span, heads + 2, HEAD)
    local_places = jnp.arange(span, dtype=jnp.int32)
    query_places = mine * span + local_places
    frequency = 10000.0 ** (-jnp.arange(ROT // 2, dtype=jnp.float32) * 2.0 / ROT)
    angles = query_places.astype(jnp.float32)[:, None] * frequency[None, :]
    cosine = jnp.cos(angles)[None, :, None, :]
    sine = jnp.sin(angles)[None, :, None, :]
    turned = rotate(project[:, :, : heads + 1], cosine, sine)
    queries = turned[:, :, :heads].astype(jnp.bfloat16)
    key_value = jnp.concatenate([turned[:, :, heads], project[:, :, heads + 1]], axis=-1).astype(
        jnp.bfloat16
    )
    fetched = [key_value]
    for offset in range(1, parts):
        fetched.append(from_behind(key_value, "seq", offset))

    def kv_at(offset):
        return fetched[offset]

    query_docs = lax.dynamic_slice_in_dim(doc_ids, mine * span, span, 1)

    def allowed(offset):
        source = mine - offset
        key_docs = lax.dynamic_slice_in_dim(doc_ids, jnp.maximum(source, 0) * span, span, 1)
        key_places = source * span + local_places
        same_doc = query_docs[:, :, None] == key_docs[:, None, :]
        causal = key_places[None, :] <= query_places[:, None]
        return (same_doc & causal[None])[:, None]

    def block_scores(offset):
        block = kv_at(offset)
        raw = (
            jnp.einsum(
                "rqhd,rkd->rhqk", queries, block[:, :, :HEAD], preferred_element_type=jnp.float32
            )
            * scale
        )
        return jnp.where(allowed(offset), raw, -jnp.inf)

    empty_scores = jnp.full((rows_here, heads, span, span), -jnp.inf, jnp.float32)
    stored = [block_scores(0)]
    for offset in range(1, parts):
        stored.append(lax.cond(mine >= offset, partial(block_scores, offset), lambda: empty_scores))
    top = jnp.max(stored[0], axis=-1)
    for offset in range(1, parts):
        top = jnp.maximum(top, jnp.max(stored[offset], axis=-1))
    total_sum = jnp.zeros_like(top)
    for offset in range(parts):
        total_sum = total_sum + jnp.sum(jnp.exp(stored[offset] - top[..., None]), axis=-1)
    log_total = top + jnp.log(total_sum)

    def block_output(offset):
        weights = jnp.exp(stored[offset] - log_total[..., None]).astype(jnp.bfloat16)
        return jnp.einsum(
            "rhqk,rkd->rqhd",
            weights,
            kv_at(offset)[:, :, HEAD:],
            preferred_element_type=jnp.float32,
        )

    zero_heads = jnp.zeros((rows_here, span, heads, HEAD), jnp.float32)
    attended = block_output(0)
    for offset in range(1, parts):
        attended = attended + lax.cond(
            mine >= offset, partial(block_output, offset), lambda: zero_heads
        )
    attended_low = attended.astype(jnp.bfloat16).reshape(count, width)
    hidden = jnp.dot(second_in, w_fc, preferred_element_type=jnp.float32) + b_fc
    act_full, gelu_pull = jax.vjp(lambda inner: jax.nn.gelu(inner, approximate=False), hidden)
    act = act_full.astype(jnp.bfloat16)
    result = tokens + jnp.dot(attended_low, w_o, preferred_element_type=jnp.float32)
    result = result + jnp.dot(act, w_proj, preferred_element_type=jnp.float32) + b_proj
    outputs = result.astype(jnp.bfloat16).reshape(rows_here, span, width)
    grad_out = cotangent.reshape(count, width)
    grad_w_proj = jnp.einsum("nf,nd->fd", act, grad_out, preferred_element_type=jnp.float32)
    grad_b_proj = jnp.sum(grad_out.astype(jnp.float32), axis=0)
    grad_act = jnp.einsum("nd,fd->nf", grad_out, w_proj, preferred_element_type=jnp.float32)
    grad_hidden = gelu_pull(grad_act)[0].astype(jnp.bfloat16)
    grad_w_fc = jnp.einsum("nd,nf->df", second_in, grad_hidden, preferred_element_type=jnp.float32)
    grad_b_fc = jnp.sum(grad_hidden.astype(jnp.float32), axis=0)
    grad_second = jnp.einsum("nf,df->nd", grad_hidden, w_fc, preferred_element_type=jnp.float32)
    grad_w_o = jnp.einsum("ne,nd->ed", attended_low, grad_out, preferred_element_type=jnp.float32)
    grad_att = jnp.einsum("nd,ed->ne", grad_out, w_o, preferred_element_type=jnp.float32)
    grad_att = grad_att.astype(jnp.bfloat16).reshape(rows_here, span, heads, HEAD)
    delta = jnp.einsum("rqhd,rqhd->rhq", grad_att.astype(jnp.float32), attended)

    def block_grads(offset):
        block = kv_at(offset)
        probs = jnp.exp(stored[offset] - log_total[..., None])
        grad_probs = jnp.einsum(
            "rqhd,rkd->rhqk", grad_att, block[:, :, HEAD:], preferred_element_type=jnp.float32
        )
        grad_scores = (probs * (grad_probs - delta[..., None])).astype(jnp.bfloat16)
        probs_low = probs.astype(jnp.bfloat16)
        part_query = (
            jnp.einsum(
                "rhqk,rkd->rqhd",
                grad_scores,
                block[:, :, :HEAD],
                preferred_element_type=jnp.float32,
            )
            * scale
        )
        part_key = (
            jnp.einsum("rhqk,rqhd->rkd", grad_scores, queries, preferred_element_type=jnp.float32)
            * scale
        )
        part_value = jnp.einsum(
            "rhqk,rqhd->rkd", probs_low, grad_att, preferred_element_type=jnp.float32
        )
        return (part_query, jnp.concatenate([part_key, part_value], axis=-1))

    zero_pair = (zero_heads, jnp.zeros((rows_here, span, 2 * HEAD), jnp.float32))
    grad_query, own_piece = block_grads(0)
    pieces = [own_piece]
    for offset in range(1, parts):
        part_query, part_kv = lax.cond(
            mine >= offset, partial(block_grads, offset), lambda: zero_pair
        )
        grad_query = grad_query + part_query
        pieces.append(part_kv)
    grad_kv = pieces[0]
    for offset in range(1, parts):
        grad_kv = grad_kv + from_behind(pieces[offset].astype(jnp.bfloat16), "seq", -offset).astype(
            jnp.float32
        )
    grad_turned = jnp.concatenate([grad_query, grad_kv[:, :, None, :HEAD]], axis=2)
    grad_project = jnp.concatenate(
        [rotate_back(grad_turned, cosine, sine), grad_kv[:, :, None, HEAD:]], axis=2
    )
    grad_project = grad_project.reshape(count, -1).astype(jnp.bfloat16)
    grad_w_qkv = jnp.einsum("nd,ne->de", first_in, grad_project, preferred_element_type=jnp.float32)
    grad_b_qkv = jnp.sum(grad_project.astype(jnp.float32), axis=0)
    grad_first = jnp.einsum("ne,de->nd", grad_project, w_qkv, preferred_element_type=jnp.float32)
    grad_gain_one = jnp.sum(normed * grad_first, axis=0)
    grad_shift_one = jnp.sum(grad_first, axis=0)
    grad_gain_two = jnp.sum(normed * grad_second, axis=0)
    grad_shift_two = jnp.sum(grad_second, axis=0)
    combined = grad_first * gain_one + grad_second * gain_two
    input_grads = grad_out.astype(jnp.float32) + norm_back(combined, normed, inverse_std)
    input_grads = input_grads.astype(jnp.bfloat16).reshape(rows_here, span, width)
    sum_a, sum_b, sum_c, sum_d, sum_e, sum_f, sum_g, sum_h, sum_i, sum_j, sum_k = (
        lax.psum_scatter(grad_w_qkv, "batch", scatter_dimension=0, tiled=True),
        lax.psum_scatter(grad_b_qkv, "batch", scatter_dimension=0, tiled=True),
        lax.psum_scatter(grad_w_o, "batch", scatter_dimension=0, tiled=True),
        lax.psum_scatter(grad_w_fc, "batch", scatter_dimension=0, tiled=True),
        lax.psum_scatter(grad_b_fc, "batch", scatter_dimension=0, tiled=True),
        lax.psum_scatter(grad_w_proj, "batch", scatter_dimension=0, tiled=True),
        lax.psum_scatter(grad_b_proj, "batch", scatter_dimension=0, tiled=True),
        lax.psum_scatter(grad_gain_one, "batch", scatter_dimension=0, tiled=True),
        lax.psum_scatter(grad_shift_one, "batch", scatter_dimension=0, tiled=True),
        lax.psum_scatter(grad_gain_two, "batch", scatter_dimension=0, tiled=True),
        lax.psum_scatter(grad_shift_two, "batch", scatter_dimension=0, tiled=True),
    )
    shards = (
        lax.psum(sum_a.astype(jnp.bfloat16), "seq").astype(jnp.float32),
        lax.psum(sum_b.astype(jnp.bfloat16), "seq").astype(jnp.float32),
        lax.psum(sum_c.astype(jnp.bfloat16), "seq").astype(jnp.float32),
        lax.psum(sum_d.astype(jnp.bfloat16), "seq").astype(jnp.float32),
        lax.psum(sum_e.astype(jnp.bfloat16), "seq").astype(jnp.float32),
        lax.psum(sum_f.astype(jnp.bfloat16), "seq").astype(jnp.float32),
        lax.psum(sum_g.astype(jnp.bfloat16), "seq").astype(jnp.float32),
        lax.psum(sum_h.astype(jnp.bfloat16), "seq").astype(jnp.float32),
        lax.psum(sum_i.astype(jnp.bfloat16), "seq").astype(jnp.float32),
        lax.psum(sum_j.astype(jnp.bfloat16), "seq").astype(jnp.float32),
        lax.psum(sum_k.astype(jnp.bfloat16), "seq").astype(jnp.float32),
    )
    return (
        outputs,
        input_grads,
        shards[0],
        shards[1],
        shards[2],
        shards[3],
        shards[4],
        shards[5],
        shards[6],
        shards[7],
        shards[8],
        shards[9],
        shards[10],
    )


def solution(mesh):
    in_specs = (
        P("batch", "seq", None),
        P("batch", None),
        P(),
        P(),
        P(),
        P(),
        P(),
        P(),
        P(),
        P(),
        P(),
        P(),
        P(),
        P("batch", "seq", None),
    )
    out_specs = (
        P("batch", "seq", None),
        P("batch", "seq", None),
        P("batch", None),
        P("batch"),
        P("batch", None),
        P("batch", None),
        P("batch"),
        P("batch", None),
        P("batch"),
        P("batch"),
        P("batch"),
        P("batch"),
        P("batch"),
    )
    return jax.shard_map(
        per_device, mesh=mesh, in_specs=in_specs, out_specs=out_specs, check_vma=False
    )
```

profile of v0, /device:TPU:0, one launch (start us, length us, event | category | flops | bytes accessed | tf_op | source)
XLA Modules:
  0.0 573.0 jit_solution(907262637779323729)
XLA Ops:
  7.3 1.4 convert_reduce_fusion.1
  8.7 1.5 fusion.130
  10.8 3.5 convolution_add_fusion
  14.3 1.8 copy.80
  17.4 1.4 slice.94
  20.8 5.8 %collective-permute-start.2 = (bf16[1,512,128]{1,2,0:T(8,128)(2,1)}, bf16[1,512,128]{1,2,0:T(8,128)(2,1)S(1)}, u32[]{:S(2)}, u32[]{:S(2)}) collective-permute-start(bf16[1,512,128]{1,2,0:T(8,128)(2,1)} %pad_maximum_fusion.7), channel_id=1, source_target_pairs={{0,24},{1,25},{2,26},{3,27},{4,28},{5,29},{6,30},{7,31}} | collective-permute-start | bytes 393224 | tf_op jit(solution)/shard_map/ppermute | solution.py:19
  26.6 1.9 collective-permute-start.1
  28.5 3.1 collective-permute-start
  32.0 6.5 %fusion.99 = (f32[12,512]{1,0:T(8,128)S(1)}, f32[512,512,12]{1,0,2:T(8,128)}) fusion(pred[512,512]{0,1:T(8,128)(4,1)S(1)} %compare_and_fusion.3, bf16[1,512,12,64]{1,3,2,0:T(8,128)(2,1)S(1)} %fusion.139, bf16[1,512,1,64]{1,3,2,0:T(8,128)(2,1)S(1)} %maximum_convert_fusion), kind=kOutput, calls=%fused_computation.119 | convolution fusion | flops 412084224 | bytes 13721600 | tf_op jit(solution)/shard_map/rqhd,rkd->rhqk/dot_general | solution.py:113
  38.5 1.7 convolution_convert_fusion
  40.2 1.4 copy.85
  41.7 2.3 conditional.9
  42.3 1.6 broadcast_in_dim.57
  44.0 4.5 copy-done.1
  48.4 6.8 %conditional.10 = (f32[1,12,512,512]{2,3,1,0:T(8,128)}, f32[12,512]{1,0:T(8,128)}, f32[1,12,512]{2,1,0:T(8,128)S(1)}) conditional(s32[]{:T(128)} %convert_element_type.232, () %tuple.82, (s32[1,512]{1,0:T(1,128)S(1)}, s32[]{:T(128)}, s32[1,2048]{1,0:T(1,128)S(1)}, s32[512]{0:T(512)S(1)}, s32[512]{0:T(512)S(1)}, ...), branch_computations={%region_6.7_spmd, %region_7.0_spmd} | conditional | flops 412871168 | bytes 14049394 | solution.py:123
  49.0 6.1 %broadcast_in_dim.60 = f32[1,12,512,512]{2,3,1,0:T(8,128)} broadcast(f32[]{:T(128)} %constant.30.clone), dimensions={} | broadcast | bytes 12582916 | tf_op jit(solution)/shard_map/broadcast_in_dim | solution.py:120
  55.9 6.7 %conditional.11 = (f32[1,12,512,512]{2,3,1,0:T(8,128)}, f32[12,512]{1,0:T(8,128)}, f32[1,12,512]{2,1,0:T(8,128)S(1)}) conditional(s32[]{:T(128)} %convert_element_type.233, () %tuple.84, (s32[1,512]{1,0:T(1,128)S(1)}, s32[]{:T(128)}, s32[1,2048]{1,0:T(1,128)S(1)}, s32[512]{0:T(512)}, s32[512]{0:T(512)S(1)}, ...), branch_computations={%region_9.10_spmd, %region_10.0_spmd} | conditional | flops 412871168 | bytes 14049394 | solution.py:123
  56.5 6.1 %broadcast_in_dim.69 = f32[1,12,512,512]{2,3,1,0:T(8,128)} broadcast(f32[]{:T(128)} %constant.42.clone), dimensions={} | broadcast | bytes 12582916 | tf_op jit(solution)/shard_map/broadcast_in_dim | solution.py:120
  64.0 18.2 %exponential_reduce_fusion.2 = (f32[12,512]{1,0:T(8,128)S(1)}, f32[12,512]{1,0:T(8,128)S(1)}, f32[12,512]{1,0:T(8,128)S(1)}, f32[12,512]{1,0:T(8,128)S(1)}) fusion(f32[1,12,512,512]{2,3,1,0:T(8,128)} %copy-done.1, f32[12,512]{1,0:T(8,128)S(1)} %maximum_maximum_fusion, f32[1,12,512,512]{2,3,1,0:T(8,128)} %get-tuple-element.194, ...), kind=kLoop, calls=%fused_computation.115 | loop fusion | flops 31432704 | bytes 50716672 | tf_op jit(solution)/shard_map/reduce_sum | solution.py:129
  82.2 9.0 %fusion.176 = f32[64,12,512]{2,0,1:T(8,128)} fusion(f32[512,512,12]{1,0,2:T(8,128)} %get-tuple-element.311, f32[12,512]{1,0:T(8,128)S(1)} %get-tuple-element.286, pred[512,512]{0,1:T(8,128)(4,1)S(1)} %compare_and_fusion.3, f32[1,512,14,64]{1,3,2,0:T(8,128)} %bitcast.508), kind=kOutput, calls=%fused_computation.235 | convolution fusion | flops 415236096 | bytes 14508032 | tf_op jit(solution)/shard_map/rhqk,rkd->rqhd/dot_general | solution.py:134
  91.2 1.5 conditional.12
  91.3 1.3 broadcast_in_dim.72
  92.8 1.4 conditional.13
  92.8 1.4 broadcast_in_dim.74
  94.2 1.3 conditional.14
  94.2 1.3 broadcast_in_dim.76
  95.6 4.6 fusion.144
  101.0 1.3 collective-permute-start.3
  104.9 2.0 conditional.17
  105.6 1.4 broadcast_in_dim.85
  106.9 1.4 collective-permute-start.5
  108.4 3.7 fusion.155
  112.3 6.8 %fusion.102 = bf16[12,512,512]{1,2,0:T(8,128)(2,1)S(1)} fusion(f32[512,512,12]{1,0,2:T(8,128)} %get-tuple-element.311, f32[12,512]{1,0:T(8,128)S(1)} %get-tuple-element.284, f32[12,512]{1,0:T(8,128)S(1)} %copy-done.27, pred[512,512]{0,1:T(8,128)(4,1)S(1)} %compare_and_fusion.3, bf16[512,12,64]{0,2,1:T(8,128)(2,1)S(1)} %bitcast.492, ...), kind=kOutput, calls=%fused_computation.122 | convolution fusion | flops 421527552 | bytes 20037632 | tf_op jit(solution)/shard_map/rqhd,rkd->rhqk/dot_general | solution.py:170
  120.3 2.0 fusion.147
  122.4 3.2 convolution_bitcast_fusion.3
  125.7 2.2 fusion.141
  127.9 14.0 %collective-permute-done.3 = bf16[1,512,128]{1,2,0:T(8,128)(2,1)} collective-permute-done((bf16[1,512,128]{1,2,0:T(8,128)(2,1)}, bf16[1,512,128]{1,2,0:T(8,128)(2,1)}, u32[]{:S(2)}, u32[]{:S(2)}) %collective-permute-start.3) | collective-permute-done | bytes 131104 | tf_op jit(solution)/shard_map/ppermute | solution.py:19
  142.0 38.2 %collective-permute-done.4 = bf16[1,512,128]{1,2,0:T(8,128)(2,1)} collective-permute-done((bf16[1,512,128]{1,2,0:T(8,128)(2,1)}, bf16[1,512,128]{1,2,0:T(8,128)(2,1)}, u32[]{:S(2)}, u32[]{:S(2)}) %collective-permute-start.4) | collective-permute-done | bytes 131104 | tf_op jit(solution)/shard_map/ppermute | solution.py:19
  180.2 38.8 %collective-permute-done.5 = bf16[1,512,128]{1,2,0:T(8,128)(2,1)S(1)} collective-permute-done((bf16[1,512,128]{1,2,0:T(8,128)(2,1)}, bf16[1,512,128]{1,2,0:T(8,128)(2,1)S(1)}, u32[]{:S(2)}, u32[]{:S(2)}) %collective-permute-start.5) | collective-permute-done | bytes 131104 | tf_op jit(solution)/shard_map/ppermute | solution.py:19
  221.4 2.9 fusion.149
  224.6 18.7 %multiply_convert_fusion = (bf16[512,3072]{1,0:T(8,128)(2,1)}, f32[512,3072]{1,0:T(8,128)S(1)}, f32[512,3072]{1,0:T(8,128)S(1)}) fusion(f32[3072]{0:T(1024)S(1)} %copy-done.31, bf16[768,3072]{1,0:T(8,128)(2,1)} %param.37, bf16[1,512,768]{2,1,0:T(8,128)(2,1)S(1)} %copy-done.3, f32[768]{0:T(1024)S(1)} %copy-done.20, f32[768]{0:T(1024)S(1)} %copy-done.21, ...), kind=kOutput, calls=%fused_computation.125 | convolution fusion | flops 2522087424 | bytes 21256192 | tf_op jit(solution)/shard_map/dot_general | solution.py:148
  243.3 6.9 %convert_reduce_fusion = (f32[3072]{0:T(1024)S(1)}, bf16[512,3072]{1,0:T(8,128)(2,1)S(1)}) fusion(f32[512,3072]{1,0:T(8,128)S(1)} %get-tuple-element.289, bf16[3072,768]{1,0:T(8,128)(2,1)} %param.39, bf16[1,512,768]{2,1,0:T(8,128)(2,1)S(1)} %copy-done.11, f32[512,3072]{1,0:T(8,128)S(1)} %get-tuple-element.309, f32[3072]{0:T(1024)S(1)} %copy-done.31), kind=kOutput, calls=%fused_computation.123 | convolution fusion | flops 2442654720 | bytes 21258240 | tf_op jit(solution)/shard_map/nd,fd->nf/dot_general | solution.py:157
  250.2 1.7 copy-done.9
  251.9 5.6 fusion.191
  257.7 8.2 %fusion.153 = f32[3072,768]{1,0:T(8,128)} fusion(bf16[512,3072]{1,0:T(8,128)(2,1)} %get-tuple-element.288, bf16[1,512,768]{2,1,0:T(8,128)(2,1)S(1)} %copy-done.11), kind=kOutput, calls=%fused_computation.202 | convolution fusion | flops 2415919104 | bytes 13369344 | tf_op jit(solution)/shard_map/nf,nd->fd/dot_general | solution.py:155
  269.2 6.1 %fusion.205 = f32[512,768]{1,0:T(8,128)S(1)} fusion(bf16[512,3072]{1,0:T(8,128)(2,1)} %get-tuple-element.288, bf16[3072,768]{1,0:T(8,128)(2,1)} %param.39), kind=kOutput, calls=%fused_computation.278 | convolution fusion | flops 2415919104 | bytes 9437184 | tf_op jit(solution)/shard_map/dot_general | solution.py:152
  275.3 1.8 fusion.145
  277.1 1.6 convert_element_type.259
  278.7 15.3 %reduce-scatter.5.cloned.1.call-done = f32[96,896]{1,0:T(8,128)} async-done(((f32[768,896]{1,0:T(8,128)}), f32[96,896]{1,0:T(8,128)}) %reduce-scatter.5.cloned.1.call-update) | async-done | bytes 344080 | tf_op jit(solution)/shard_map/reduce_scatter | solution.py:223
  294.0 1.7 convert_element_type.254
  295.7 99.3 %reduce-scatter.9.cloned.1.call-done = f32[96,3072]{1,0:T(8,128)} async-done(((f32[768,3072]{1,0:T(8,128)}), f32[96,3072]{1,0:T(8,128)}) %reduce-scatter.9.cloned.1.call-update) | async-done | bytes 1179664 | tf_op jit(solution)/shard_map/reduce_scatter | solution.py:226
  395.0 2.2 convert_element_type.261
  397.2 98.0 %reduce-scatter.11.cloned.1.call-done = f32[384,768]{1,0:T(8,128)} async-done(((f32[3072,768]{1,0:T(8,128)}), f32[384,768]{1,0:T(8,128)}) %reduce-scatter.11.cloned.1.call-update) | async-done | bytes 1179664 | tf_op jit(solution)/shard_map/reduce_scatter | solution.py:228
  495.2 2.1 convert_element_type.266
  497.4 3.4 fusion.206
  500.8 7.5 %fusion.195 = (f32[768]{0:T(1024)S(1)}, f32[768]{0:T(1024)S(1)}, f32[512]{0:T(512)S(1)}, f32[512]{0:T(512)S(1)}, f32[512,768]{1,0:T(8,128)S(1)}, /*index=5*/f32[768]{0:T(1024)S(1)}, f32[768]{0:T(1024)S(1)}) fusion(f32[512]{0:T(512)S(1)} %copy-done.23, f32[512]{0:T(512)S(1)} %copy-done.19, bf16[1,512,768]{2,1,0:T(8,128)(2,1)S(1)} %copy-done.3, ...), kind=kOutput, calls=%fused_computation.271 | convolution fusion | flops 2421813248 | bytes 11823104 | tf_op jit(solution)/shard_map/nf,df->nd/dot_general | solution.py:161
  508.4 1.6 convert_reduce_fusion.2
  509.9 26.3 %all-reduce.7 = (bf16[896]{0:T(1024)(128)(2,1)S(1)}, bf16[3072]{0:T(1024)(128)(2,1)S(1)}, bf16[768]{0:T(1024)(128)(2,1)S(1)}, bf16[768]{0:T(1024)(128)(2,1)S(1)}...) all-reduce(f32[896]{0:T(1024)S(1)} %reduce_sum.146, ...), channel_id=3, replica_groups=mesh['seq'=4,'batch'=8] {'batch'}, use_global_device_ids=true, to_apply=%region_33.34.clone | all-reduce | flops 7808 | bytes 46848
  536.8 9.8 %all-reduce.8 = (bf16[112]{0:T(256)(128)(2,1)S(1)}, bf16[384]{0:T(512)(128)(2,1)S(1)}, bf16[96]{0:T(256)(128)(2,1)S(1)}, bf16[96]{0:T(256)(128)(2,1)S(1)}, bf16[...) all-reduce(bf16[112]{0:T(256)(128)(2,1)S(1)} %dynamic-slice.27, ...), channel_id=1, replica_groups=mesh['seq'=4,'batch'=8] {'seq'}, use_global_device_ids=true, to_apply=%region_34.35 | all-reduce | flops 976 | bytes 3904 | tf_op jit(solution)/shard_map/psum | solution.py:237
  550.2 8.1 %all-reduce.12.cloned.1.call-done = (bf16[96,896]{1,0:T(8,128)(2,1)}, bf16[96,768]{1,0:T(8,128)(2,1)}, bf16[96,3072]{1,0:T(8,128)(2,1)}, bf16[384,768]{1,0:T(8,128)(2,1)}) async-done(((bf16[96,896]{1,0:T(8,128)(2,1)}, bf16[96,768]{1,0:T(8,128)(2,1)}, bf16[96,3072]{1,0:T(8,128)(2,1)}, bf16[384,768]{1,0:T(8,128)(2,1)}), (bf16[96,896]{1,0:T(8,128)(2,1)}, bf16[96,768]{1,0:T(8,128)(2,1)}, ...) | async-done | bytes 1499152 | tf_op jit(solution)/shard_map/psum | solution.py:236
  558.4 1.7 convert_element_type.255
  560.0 1.6 convert_element_type.260
  561.7 2.2 convert_element_type.262
  563.9 2.2 convert_element_type.267
  (146 shorter events, 23.8 us)
Async XLA Ops:
  7.2 3.6 copy-start
  7.2 269.9 %reduce-scatter.7.cloned.1.call-start = ((), (), s32[]{:S(2)}) async-start(), calls=%async_computation.5 | async-start | bytes 2654208 | tf_op jit(solution)/shard_map/reduce_scatter | solution.py:225
  8.7 1.5 copy-start.18
  10.2 0.6 copy-start.22
  10.8 20.9 %copy-start.28 = (s32[1,2048]{1,0:T(1,128)S(1)}, s32[1,2048]{1,0:T(1,128)}, u32[]{:S(2)}) copy-start(s32[1,2048]{1,0:T(1,128)} %param.33) | copy-start | bytes 24580
  16.1 1.3 copy-start.8
  19.0 1.1 copy-start.14
  19.0 1.8 copy-start.16
  20.8 34.5 %collective-permute-start.2 = (bf16[1,512,128]{1,2,0:T(8,128)(2,1)}, bf16[1,512,128]{1,2,0:T(8,128)(2,1)S(1)}, u32[]{:S(2)}, u32[]{:S(2)}) collective-permute-start(bf16[1,512,128]{1,2,0:T(8,128)(2,1)} %pad_maximum_fusion.7), channel_id=1, source_target_pairs={{0,24},{1,25},{2,26},{3,27},{4,28},{5,29},{6,30},{7,31}} | collective-permute-start | bytes 393224 | tf_op jit(solution)/shard_map/ppermute | solution.py:19
  26.6 17.4 %collective-permute-start.1 = (bf16[1,512,128]{1,2,0:T(8,128)(2,1)}, bf16[1,512,128]{1,2,0:T(8,128)(2,1)}, u32[]{:S(2)}, u32[]{:S(2)}) collective-permute-start(bf16[1,512,128]{1,2,0:T(8,128)(2,1)} %pad_maximum_fusion.7), channel_id=1, source_target_pairs={{0,16},{8,24},{1,17},{9,25},{2,18},{10,26},{3,19},{11,27},{4,20},{... | collective-permute-start | bytes 393224 | tf_op jit(solution)/shard_map/ppermute | solution.py:19
  28.5 13.1 %collective-permute-start = (bf16[1,512,128]{1,2,0:T(8,128)(2,1)}, bf16[1,512,128]{1,2,0:T(8,128)(2,1)}, u32[]{:S(2)}, u32[]{:S(2)}) collective-permute-start(bf16[1,512,128]{1,2,0:T(8,128)(2,1)} %pad_maximum_fusion.7), channel_id=1, source_target_pairs={{0,8},{8,16},{16,24},{1,9},{9,17},{17,25},{2,10},{10,18},{18,26},{... | collective-permute-start | bytes 393224 | tf_op jit(solution)/shard_map/ppermute | solution.py:19
  32.0 6.5 %copy-start.10 = (bf16[1,512,768]{2,1,0:T(8,128)(2,1)S(1)}, bf16[1,512,768]{2,1,0:T(8,128)(2,1)}, u32[]{:S(2)}) copy-start(bf16[1,512,768]{2,1,0:T(8,128)(2,1)} %param.45) | copy-start | bytes 2359300
  32.0 6.5 %copy-start.29 = (bf16[768,768]{1,0:T(8,128)(2,1)S(1)}, bf16[768,768]{1,0:T(8,128)(2,1)}, u32[]{:S(2)}) copy-start(bf16[768,768]{1,0:T(8,128)(2,1)} %param.36) | copy-start | bytes 3538948
  43.9 4.5 copy-start.1
  62.6 0.6 copy-start.24
  82.2 9.0 %copy-start.26 = (f32[12,512]{1,0:T(8,128)}, f32[12,512]{1,0:T(8,128)S(1)}, u32[]{:S(2)}) copy-start(f32[12,512]{1,0:T(8,128)S(1)} %get-tuple-element.286) | copy-start | bytes 73732
  82.2 9.0 %copy-start.25 = (f32[1,12,512]{2,1,0:T(8,128)S(1)}, f32[1,12,512]{2,1,0:T(8,128)}, u32[]{:S(2)}) copy-start(f32[1,12,512]{2,1,0:T(8,128)} %copy-done.24) | copy-start | bytes 73732
  101.0 1.3 copy-start.4
  101.0 41.0 %collective-permute-start.3 = (bf16[1,512,128]{1,2,0:T(8,128)(2,1)}, bf16[1,512,128]{1,2,0:T(8,128)(2,1)}, u32[]{:S(2)}, u32[]{:S(2)}) collective-permute-start(bf16[1,512,128]{1,2,0:T(8,128)(2,1)} %get-tuple-element.202), channel_id=1, source_target_pairs={{8,0},{16,8},{24,16},{9,1},{17,9},{25,17},{10,2},{18,10},{26,18},{... | collective-permute-start | bytes 393224 | tf_op jit(solution)/shard_map/ppermute | solution.py:19
  103.6 1.3 copy-start.6
  103.6 76.6 %collective-permute-start.4 = (bf16[1,512,128]{1,2,0:T(8,128)(2,1)}, bf16[1,512,128]{1,2,0:T(8,128)(2,1)}, u32[]{:S(2)}, u32[]{:S(2)}) collective-permute-start(bf16[1,512,128]{1,2,0:T(8,128)(2,1)} %get-tuple-element.203), channel_id=1, source_target_pairs={{16,0},{24,8},{17,1},{25,9},{18,2},{26,10},{19,3},{27,11},{20,4},{... | collective-permute-start | bytes 393224 | tf_op jit(solution)/shard_map/ppermute | solution.py:19
  106.9 5.3 copy-start.27
  106.9 112.0 %collective-permute-start.5 = (bf16[1,512,128]{1,2,0:T(8,128)(2,1)}, bf16[1,512,128]{1,2,0:T(8,128)(2,1)S(1)}, u32[]{:S(2)}, u32[]{:S(2)}) collective-permute-start(bf16[1,512,128]{1,2,0:T(8,128)(2,1)} %get-tuple-element.204), channel_id=1, source_target_pairs={{24,0},{25,1},{26,2},{27,3},{28,4},{29,5},{30,6},{31,7}} | collective-permute-start | bytes 393224 | tf_op jit(solution)/shard_map/ppermute | solution.py:19
  112.1 181.9 %reduce-scatter.5.cloned.1.call-start = ((), (), s32[]{:S(2)}) async-start(), calls=%async_computation.4 | async-start | bytes 3096576 | tf_op jit(solution)/shard_map/reduce_scatter | solution.py:223
  112.3 10.0 %slice-start = ((s8[12582912]{0:T(1024)(128)(4,1)}), s8[4194304]{0:T(1024)(128)(4,1)S(1)}, s32[]{:S(2)}) async-start(s8[12582912]{0:T(1024)(128)(4,1)} %bitcast.494), calls=%async_computation.9 | async-start | bytes 8388608
  112.3 10.0 %slice-start.1 = ((s8[12582912]{0:T(1024)(128)(4,1)}), s8[4194304]{0:T(1024)(128)(4,1)S(1)}, s32[]{:S(2)}) async-start(s8[12582912]{0:T(1024)(128)(4,1)} %bitcast.494), calls=%async_computation.10 | async-start | bytes 8388608
  119.1 3.3 slice-start.2
  122.4 3.3 copy-start.5
  122.4 3.3 copy-start.7
  125.6 94.5 %copy-start.15 = (f32[512,8]{0,1:T(8,128)S(1)}, f32[512,8]{0,1:T(8,128)}, u32[]{:S(2)}) copy-start(f32[512,8]{0,1:T(8,128)} %copy-done.14) | copy-start | bytes 49156
  125.6 94.5 %copy-start.17 = (f32[512,8]{0,1:T(8,128)S(1)}, f32[512,8]{0,1:T(8,128)}, u32[]{:S(2)}) copy-start(f32[512,8]{0,1:T(8,128)} %copy-done.16) | copy-start | bytes 49156
  125.6 95.7 %copy-start.3 = (bf16[1,512,768]{2,1,0:T(8,128)(2,1)S(1)}, bf16[1,512,768]{2,1,0:T(8,128)(2,1)}, u32[]{:S(2)}) copy-start(bf16[1,512,768]{2,1,0:T(8,128)(2,1)} %param.32) | copy-start | bytes 2359300
  125.7 95.7 %copy-start.19 = (f32[512]{0:T(512)S(1)}, f32[512]{0:T(512)}, u32[]{:S(2)}) copy-start(f32[512]{0:T(512)} %copy-done.18) | copy-start | bytes 6148
  125.7 95.7 %copy-start.23 = (f32[512]{0:T(512)S(1)}, f32[512]{0:T(512)}, u32[]{:S(2)}) copy-start(f32[512]{0:T(512)} %copy-done.22) | copy-start | bytes 6148
  125.7 95.7 %copy-start.32 = (f32[768]{0:T(1024)S(1)}, f32[768]{0:T(1024)}, u32[]{:S(2)}) copy-start(f32[768]{0:T(1024)} %param.42) | copy-start | bytes 9220
  125.7 95.7 %copy-start.34 = (f32[768]{0:T(1024)S(1)}, f32[768]{0:T(1024)}, u32[]{:S(2)}) copy-start(f32[768]{0:T(1024)} %param.41) | copy-start | bytes 9220
  220.1 4.4 copy-start.20
  220.1 4.4 copy-start.21
  220.2 4.4 copy-start.31
  220.4 0.9 copy-start.13
  224.3 19.0 %copy-start.11 = (bf16[1,512,768]{2,1,0:T(8,128)(2,1)S(1)}, bf16[1,512,768]{2,1,0:T(8,128)(2,1)}, u32[]{:S(2)}) copy-start(bf16[1,512,768]{2,1,0:T(8,128)(2,1)} %param.45) | copy-start | bytes 2359300
  224.3 170.7 %reduce-scatter.9.cloned.1.call-start = ((), (), s32[]{:S(2)}) async-start(), calls=%async_computation.6 | async-start | bytes 10616832 | tf_op jit(solution)/shard_map/reduce_scatter | solution.py:226
  250.2 1.7 copy-start.9
  257.4 237.8 %reduce-scatter.11.cloned.1.call-start = ((), (), s32[]{:S(2)}) async-start(), calls=%async_computation.7 | async-start | bytes 10616832 | tf_op jit(solution)/shard_map/reduce_scatter | solution.py:228
  265.9 0.7 copy-start.35
  266.0 292.4 %all-reduce.12.cloned.1.call-start = ((), (), s32[]{:S(2)}) async-start(), calls=%async_computation.8 | async-start | bytes 2998272 | tf_op jit(solution)/shard_map/psum | solution.py:236
  269.1 6.2 %copy-start.12 = (bf16[1,512,12,64]{1,3,2,0:T(8,128)(2,1)S(1)}, bf16[1,512,12,64]{1,3,2,0:T(8,128)(2,1)}, u32[]{:S(2)}) copy-start(bf16[1,512,12,64]{1,3,2,0:T(8,128)(2,1)} %get-tuple-element.285) | copy-start | bytes 2359300
  269.1 6.2 %copy-start.30 = (bf16[768,768]{1,0:T(8,128)(2,1)S(1)}, bf16[768,768]{1,0:T(8,128)(2,1)}, u32[]{:S(2)}) copy-start(bf16[768,768]{1,0:T(8,128)(2,1)} %param.36) | copy-start | bytes 3538948
  269.2 6.2 %copy-start.33 = (f32[768]{0:T(1024)S(1)}, f32[768]{0:T(1024)}, u32[]{:S(2)}) copy-start(f32[768]{0:T(1024)} %param.40) | copy-start | bytes 9220
Sparse Core Ops, SparseCore 0:
  112.2 142.0 reduce-scatter.6
  256.5 37.4 reduce-scatter.4
  296.4 98.5 reduce-scatter.8
  397.3 97.8 reduce-scatter.10
  499.5 58.8 all-reduce.11
where the time goes:
time: 582 us; the launch traced here: 573 us
  waiting for transfers between devices  312 us (54%)
  matrix products  98.6 us (17%)
  other arithmetic  52.8 us (9%)
  local copies, waits for them, and re-layouts  40.1 us (7%)
  blocking collectives  36.1 us (6%)
  between operations  16.9 us (3%)
  starting transfers between devices  15.7 us (3%)
    reduce_scatter x1, waiting for transfers between devices, per_device(): lax.psum_scatter(grad_w_fc, 'batch', scatter_dimension=0, tiled=True)  99.3 us
    reduce_scatter x1, waiting for transfers between devices, per_device(): lax.psum_scatter(grad_w_proj, 'batch', scatter_dimension=0, tiled=True)  98 us
    ppermute x6, waiting for transfers between devices, from_behind(): return lax.ppermute(block, axis, route)  91 us
    unnamed x1, blocking collectives  26.3 us
    dot_general x1, matrix products, per_device(): hidden = jnp.dot(second_in, w_fc, preferred_element_type=jnp.float32) + b_fc  18.7 us
    reduce_sum x1, other arithmetic, per_device(): jnp.sum(jnp.exp(stored[offset] - top[..., None]), axis=-1)  18.2 us
    reduce_scatter x1, waiting for transfers between devices, per_device(): lax.psum_scatter(grad_w_qkv, 'batch', scatter_dimension=0, tiled=True)  15.3 us
    ppermute x6, starting transfers between devices, from_behind(): return lax.ppermute(block, axis, route)  14.8 us
  transfers between devices with their start and end apart: 11, of which 7 were waited for; matrix products, arithmetic and copies ran while one was open for 20% of the time, Pallas kernels for 0%

commit v1 on v0

v1 whole, which is shorter than its diff:
```python
import functools
import math
import types

import jax
import jax.numpy as jnp
import numpy as np
from jax import lax
from jax.experimental import pallas as pl
from jax.experimental.pallas import tpu as pltpu
from jax.sharding import PartitionSpec as P

HEAD = 64
ROT = 16
EPSILON = 1e-05
LANES = 128
BLOCK = 256
FAR = -1e30
LOG2E = math.log2(math.e)
MESH = pl.DeviceIdType.MESH
F32 = jnp.float32
BF16 = jnp.bfloat16

CHUNKS = 8


def mm(a, b, ca=1, cb=0):
    return lax.dot_general(a, b, (((ca,), (cb,)), ((), ())), preferred_element_type=F32)


def flip(value):
    return value.astype(F32).T


def lanes_of(shape):
    return lax.broadcasted_iota(jnp.int32, shape, 1)


def rows_of(shape):
    return lax.broadcasted_iota(jnp.int32, shape, 0)


def gelu_parts(hidden):
    size = jnp.abs(hidden)
    t = pl.reciprocal(1.0 + (0.3275911 / math.sqrt(2.0)) * size)
    bell = jnp.exp2(hidden * hidden * (-0.5 * LOG2E))
    poly = 0.5 * 1.061405429
    for term in (-1.453152027, 1.421413741, -0.284496736, 0.254829592):
        poly = poly * t + 0.5 * term
    tail = poly * t * bell
    below = jnp.where(hidden >= 0, 1.0 - tail, tail)
    return below, hidden * bell * (1.0 / math.sqrt(2.0 * math.pi))


def layer_kernel(names, parts, inside, *refs):
    r = types.SimpleNamespace(**dict(zip(names, refs, strict=True)))
    span, width = r.x.shape
    hidden_units = r.wfc.shape[1]
    heads = width // HEAD
    mine = lax.axis_index("seq")
    batch = lax.axis_index("batch")
    core = lax.rem(batch, 2)

    loads = [
        pltpu.make_async_copy(src, dst, r.load_sem.at[i])
        for i, (src, dst) in enumerate(
            [(r.x_h, r.x), (r.wq_h, r.wq), (r.cot_h, r.cot), (r.wo_h, r.wo), (r.wfc_h, r.wfc), (r.wp_h, r.wp)]
        )
    ]
    for load in loads:
        load.start()

    barrier = pltpu.get_barrier_semaphore()
    for distance in range(1, parts):
        pl.semaphore_signal(
            barrier, inc=1, device_id=(lax.rem(mine + distance, parts), batch), device_id_type=MESH
        )
    pl.semaphore_wait(barrier, parts - 1)

    loads[0].wait()

    def norm_tile(i):
        tokens = r.x[pl.ds(i * LANES, LANES), :].astype(F32)
        average = jnp.mean(tokens, axis=-1, keepdims=True)
        centered = tokens - average
        variance = jnp.mean(centered * centered, axis=-1, keepdims=True)
        inverse_std = lax.rsqrt(variance + EPSILON)
        return centered * inverse_std, inverse_std

    for i in range(span // LANES):
        normed, _ = norm_tile(i)
        rows = pl.ds(i * LANES, LANES)
        first = normed * r.g1[...] + r.s1[...]
        second = normed * r.g2[...] + r.s2[...]
        r.fi[rows, :] = first.astype(BF16)
        r.si[rows, :] = second.astype(BF16)
        r.fit[:, rows] = first.T.astype(BF16)
        r.sit[:, rows] = second.T.astype(BF16)

    half = ROT // 2
    index = rows_of((half, span))
    frequency = jnp.zeros((half, span), F32)
    for i in range(half):
        frequency = jnp.where(index == i, np.float32(10000.0 ** (-2.0 * i / ROT)), frequency)
    angle = (mine * span + lanes_of((half, span))).astype(F32) * frequency
    cosine, sine = jnp.cos(angle), jnp.sin(angle)
    r.cos[...] = cosine
    r.sin[...] = sine
    ones = jnp.ones((HEAD - ROT, span), F32)
    zeros = jnp.zeros((HEAD - ROT, span), F32)
    table_cos = jnp.concatenate([cosine, cosine, ones] * 2, axis=0).T
    table_sin = jnp.concatenate([-sine, sine, zeros] * 2, axis=0).T
    lane = lanes_of((span, LANES))

    def rotate(tile, cos_of, sin_of):
        partner = jnp.where(
            lax.rem(lane, HEAD) < half, pltpu.roll(tile, LANES - half, 1), pltpu.roll(tile, half, 1)
        )
        return tile * cos_of + partner * sin_of

    def docs_row(distance):
        part = jnp.maximum(mine - distance, 0)
        return r.docs[0:1, pl.ds(pl.multiple_of(part * span, LANES), span)]

    loads[1].wait()
    key_value = mm(r.fi[...], r.wq[:, width:]) + r.bq[:, width:]
    low = lane < HEAD
    key_value = rotate(key_value, jnp.where(low, table_cos, 1.0), jnp.where(low, table_sin, 0.0))
    r.kv[0] = key_value.astype(BF16)
    for distance in range(1, parts):

        @pl.when(mine + distance < parts)
        def _():
            kv_copy(r, mine, batch, parts, distance).start()

    feature_row = rows_of((LANES, span)) - HEAD
    query_feature = jnp.where(feature_row == docs_row(0), 1.0, 0.0).T
    for i in range(heads // 2):
        columns = slice(i * LANES, (i + 1) * LANES)
        tile = mm(r.fi[...], r.wq[:, columns]) + r.bq[:, columns]
        tile = rotate(tile, table_cos, table_sin) * (LOG2E / math.sqrt(HEAD))
        r.q[2 * i] = jnp.where(low, tile, query_feature).astype(BF16)
        r.q[2 * i + 1] = jnp.where(low, pltpu.roll(tile, HEAD, 1), query_feature).astype(BF16)

    loads[2].wait()
    loads[3].wait()
    for i in range(width // BLOCK):
        rows = slice(i * BLOCK, (i + 1) * BLOCK)
        r.dot[rows, :] = mm(r.wo[rows, :], r.cot[...], 1, 1).astype(BF16)

    loads[4].wait()
    loads[5].wait()
    r.result[...] = jnp.zeros_like(r.result)
    r.second[...] = jnp.zeros_like(r.second)
    ones_rows = jnp.ones((8, span), BF16)
    group = 2 * 4 * 96

    def feed_forward(g, _):
        columns = pl.ds(pl.multiple_of(g * group, LANES), group)
        hidden = mm(r.si[...], r.wfc[:, columns]) + r.bfc[:, columns]
        grad_act = mm(r.cot[...], r.wp[columns, :], 1, 1)
        below, slope = gelu_parts(hidden)
        r.act[...] = (hidden * below).astype(BF16)
        r.gh[...] = (grad_act * (below + slope)).astype(BF16)
        grad_w = mm(r.sit[...], r.gh[...])
        for k in range(group // BLOCK):
            place = g * (group // BLOCK) + k
            for b in range(8):
                r.grads[place // 4, b % 2, lax.rem(place, 4) // 2, lax.rem(place, 2), b // 2] = grad_w[
                    b * 96 : (b + 1) * 96, k * BLOCK : (k + 1) * BLOCK
                ].astype(BF16)
        grad_w = mm(r.act[...], r.cot[...], 0, 0)
        for k in range(3):
            for c in range(2):
                for q in range(4):
                    row = (c * 4 + q) * 96
                    r.grads[3 + k, c, q // 2, q % 2, g] = grad_w[
                        row : row + 96, k * BLOCK : (k + 1) * BLOCK
                    ].astype(BF16)
        r.sum_fc[:, columns] = mm(ones_rows, r.gh[...])
        r.result[...] += mm(r.act[...], r.wp[columns, :])
        r.second[...] += mm(r.gh[...], r.wfc[:, columns], 1, 1)
        return 0

    lax.fori_loop(0, hidden_units // group, feed_forward, 0)

    for distance in range(parts):

        @pl.when(mine >= distance)
        def _():
            if distance:
                kv_copy(r, mine, batch, parts, distance).wait_recv()
            docs = docs_row(distance)
            apart = (feature_row >= 0) & (feature_row < 8) & (feature_row != docs)
            key_feature = jnp.where(apart, FAR, 0.0).T
            pair = r.kv[distance].astype(F32)
            keys = jnp.where(low, pair, key_feature)
            values = jnp.where(low, pltpu.roll(pair, HEAD, 1), jnp.where(lane < HEAD + 2, 1.0, 0.0))
            r.kx[distance] = keys.astype(BF16)
            r.kxt[distance] = keys.T.astype(BF16)
            r.vx[distance] = values.astype(BF16)
            r.vxt[distance] = values.T.astype(BF16)

    r.dk[...] = jnp.zeros_like(r.dk)
    r.dv[...] = jnp.zeros_like(r.dv)

    def one_head(h, _):
        rows = pl.ds(pl.multiple_of(h * HEAD, HEAD), HEAD)

        def scores(distance, causal):
            raw = mm(r.kx[distance], r.q[h], 1, 1)
            if causal:
                raw = jnp.where(rows_of(raw.shape) <= lanes_of(raw.shape), raw, FAR)
            r.scores[distance] = raw
            return jnp.max(raw, axis=0, keepdims=True)

        top = scores(0, True)
        top = lax.fori_loop(1, mine + 1, lambda d, m: jnp.maximum(m, scores(d, False)), top)
        r.att[...] = jnp.zeros_like(r.att)

        def weigh(distance, _):
            raised = jnp.exp2(r.scores[distance] - top).astype(BF16)
            r.raised[distance] = raised
            r.att[...] += mm(r.vxt[distance], raised)
            return 0

        lax.fori_loop(0, mine + 1, weigh, 0)
        inverse = 1.0 / r.att[HEAD : HEAD + 1, :]
        attended = r.att[:HEAD, :] * inverse
        r.attt[rows, :] = attended.astype(BF16)
        grad_att = r.dot[rows, :].astype(F32)
        delta = jnp.sum(grad_att * attended, axis=0, keepdims=True) * -inverse
        delta_high = delta.astype(BF16).astype(F32)
        row = rows_of((HEAD, span))
        extra = jnp.where(row == 0, delta_high, jnp.where(row == 1, delta - delta_high, 0.0))
        grad_att = jnp.concatenate([grad_att * inverse, extra], axis=0)
        r.ga[...] = grad_att.astype(BF16)
        r.gat[...] = grad_att.T.astype(BF16)
        r.dq[...] = jnp.zeros_like(r.dq)

        def back(distance, _):
            grad_probs = mm(r.vx[distance], r.ga[...])
            raised = r.raised[distance]
            grad_scores = (raised.astype(F32) * grad_probs).astype(BF16)
            r.dv[distance] += mm(raised, r.gat[...])
            r.dk[distance] += mm(grad_scores, r.q[h])
            r.dq[...] += mm(r.kxt[distance], grad_scores)
            return 0

        lax.fori_loop(0, mine + 1, back, 0)
        r.gpt[rows, :] = rotate_back(r, r.dq[:HEAD, :] * (1.0 / math.sqrt(HEAD))).astype(BF16)
        return 0

    lax.fori_loop(0, heads, one_head, 0)

    def packed(distance):
        return jnp.where(low, r.dk[distance] * (1.0 / LOG2E), pltpu.roll(r.dv[distance], HEAD, 1))

    for distance in range(1, parts):

        @pl.when(mine >= distance)
        def _():
            r.dkv_out[distance] = packed(distance).astype(BF16)
            dkv_copy(r, mine, batch, parts, distance).start()

    grad_w = mm(r.attt[...], r.cot[...])
    for b in range(8):
        for q in range(4):
            piece = grad_w[b * 96 : (b + 1) * 96, q * 192 : (q + 1) * 192]
            piece = jnp.concatenate([piece, jnp.zeros((96, 64), F32)], axis=1)
            r.grads[6, b % 2, q // 2, q % 2, b // 2] = piece.astype(BF16)

    r.total[...] = packed(0)
    for distance in range(1, parts):

        @pl.when(mine + distance < parts)
        def _():
            dkv_copy(r, mine, batch, parts, distance).wait_recv()
            r.total[...] += r.dkv_in[distance].astype(F32)

    pair = r.total[...].T
    r.gpt[width : width + HEAD, :] = rotate_back(r, pair[:HEAD]).astype(BF16)
    r.gpt[width + HEAD :, :] = pair[HEAD:].astype(BF16)

    grad_w = mm(r.fit[...], r.gpt[...], 1, 1)
    for b in range(8):
        for q in range(4):
            piece = grad_w[b * 96 : (b + 1) * 96, q * BLOCK : min((q + 1) * BLOCK, width + 2 * HEAD)]
            if q == 3:
                piece = jnp.concatenate([piece, jnp.zeros((96, LANES), F32)], axis=1)
            r.grads[7, b % 2, q // 2, q % 2, b // 2] = piece.astype(BF16)
    for i in range((width + 2 * HEAD) // LANES):
        columns = slice(i * LANES, (i + 1) * LANES)
        r.gp[:, columns] = flip(r.gpt[columns, :]).astype(BF16)

    r.first[...] = mm(r.gp[...], r.wq[...], 1, 1)
    sums = [jnp.zeros((1, width), F32) for _ in range(4)]
    for i in range(span // LANES):
        rows = pl.ds(i * LANES, LANES)
        normed, inverse_std = norm_tile(i)
        first, second = r.first[rows, :], r.second[rows, :]
        for j, term in enumerate((normed * first, first, normed * second, second)):
            sums[j] = sums[j] + jnp.sum(term, axis=0, keepdims=True)
        scaled = first * r.g1[...] + second * r.g2[...]
        mean_one = jnp.mean(scaled, axis=-1, keepdims=True)
        mean_two = jnp.mean(scaled * normed, axis=-1, keepdims=True)
        back = inverse_std * (scaled - mean_one - normed * mean_two)
        r.input_grads[rows, :] = (r.cot[rows, :].astype(F32) + back).astype(BF16)

    sum_qkv = mm(ones_rows, r.gpt[...], 1, 1)[0:1]
    sum_proj = mm(ones_rows, r.cot[...])[0:1]
    for b in range(8):
        lines = [cut(sum_qkv, b * 112, 112)]
        lines += [r.sum_fc[0:1, b * 384 + i * LANES : b * 384 + (i + 1) * LANES] for i in range(3)]
        lines += [cut(line, b * 96, 96) for line in (sum_proj, *sums)]
        lines.append(jnp.zeros((16 - len(lines), LANES), F32))
        r.grads[7, b % 2, 1, 1, b // 2, 0:16, LANES:] = jnp.concatenate(lines, axis=0).astype(BF16)

    for i in range(width // LANES):
        columns = slice(i * LANES, (i + 1) * LANES)
        r.fi[:, columns] = flip(r.attt[columns, :]).astype(BF16)
    r.outputs[...] = (r.result[...] + r.x[...].astype(F32) + r.bp[...] + mm(r.fi[...], r.wo[...])).astype(BF16)

    copy = pltpu.make_async_copy(r.grads, r.grads_out, r.load_sem.at[0])
    copy.start()
    copy.wait()
    for distance in range(1, parts):

        @pl.when(mine + distance < parts)
        def _():
            kv_copy(r, mine, batch, parts, distance).wait_send()

        @pl.when(mine >= distance)
        def _():
            dkv_copy(r, mine, batch, parts, distance).wait_send()


def cut(line, start, size):
    line = jnp.concatenate([line, jnp.zeros((1, LANES), F32)], axis=1)
    base = start // LANES * LANES
    line = line[:, base : base + 2 * LANES]
    shift = start - base
    if shift:
        line = pltpu.roll(line, 2 * LANES - shift, 1)
    return jnp.where(lanes_of((1, LANES)) < size, line[:, :LANES], 0.0)


def rotate_back(r, grads):
    half = ROT // 2
    one, two = grads[:half], grads[half:ROT]
    cosine, sine = r.cos[...], r.sin[...]
    return jnp.concatenate([one * cosine + two * sine, two * cosine - one * sine, grads[ROT:]], axis=0)


def kv_copy(r, mine, batch, parts, distance):
    return pltpu.make_async_remote_copy(
        src_ref=r.kv.at[0],
        dst_ref=r.kv.at[distance],
        send_sem=r.kv_sem.at[0, distance],
        recv_sem=r.kv_sem.at[1, distance],
        device_id=(lax.rem(mine + distance, parts), batch),
        device_id_type=MESH,
    )


def dkv_copy(r, mine, batch, parts, distance):
    return pltpu.make_async_remote_copy(
        src_ref=r.dkv_out.at[distance],
        dst_ref=r.dkv_in.at[distance],
        send_sem=r.dkv_sem.at[0, distance],
        recv_sem=r.dkv_sem.at[1, distance],
        device_id=(lax.rem(mine - distance + parts, parts), batch),
        device_id_type=MESH,
    )


def per_device(inputs, doc_ids, w_qkv, b_qkv, w_o, w_fc, b_fc, w_proj, b_proj, gain_one, shift_one, gain_two, shift_two, cotangent):
    rows_here, span, width = inputs.shape
    assert rows_here == 1
    parts = lax.axis_size("seq")
    heads = width // HEAD
    hidden_units = w_fc.shape[1]
    merged = width + 2 * HEAD
    inside = False
    vmem = pl.BlockSpec(memory_space=pltpu.VMEM)
    anywhere = pl.BlockSpec(memory_space=pl.ANY)

    small = dict(docs=doc_ids, bq=b_qkv, bfc=b_fc, bp=b_proj, g1=gain_one, s1=shift_one, g2=gain_two, s2=shift_two)
    small = {name: value.reshape(1, -1) for name, value in small.items()}
    large = dict(x_h=inputs[0], cot_h=cotangent[0], wq_h=w_qkv, wo_h=w_o, wfc_h=w_fc, wp_h=w_proj)
    grads_shape = (CHUNKS, 2, 2, 2, 4, 96, BLOCK)
    outs = dict(
        outputs=(jax.ShapeDtypeStruct((span, width), BF16), vmem),
        input_grads=(jax.ShapeDtypeStruct((span, width), BF16), vmem),
        grads_out=(jax.ShapeDtypeStruct(grads_shape, BF16), anywhere),
    )
    scratch = dict(
        x=pltpu.VMEM((span, width), BF16),
        cot=pltpu.VMEM((span, width), BF16),
        wq=pltpu.VMEM((width, merged), BF16),
        wo=pltpu.VMEM((width, width), BF16),
        wfc=pltpu.VMEM((width, hidden_units), BF16),
        wp=pltpu.VMEM((hidden_units, width), BF16),
        fi=pltpu.VMEM((span, width), BF16),
        si=pltpu.VMEM((span, width), BF16),
        fit=pltpu.VMEM((width, span), BF16),
        sit=pltpu.VMEM((width, span), BF16),
        cos=pltpu.VMEM((ROT // 2, span), F32),
        sin=pltpu.VMEM((ROT // 2, span), F32),
        kv=pltpu.VMEM((parts, span, LANES), BF16),
        q=pltpu.VMEM((heads, span, LANES), BF16),
        dot=pltpu.VMEM((width, span), BF16),
        act=pltpu.VMEM((span, width), BF16),
        gh=pltpu.VMEM((span, width), BF16),
        result=pltpu.VMEM((span, width), F32),
        second=pltpu.VMEM((span, width), F32),
        first=pltpu.VMEM((span, width), F32),
        sum_fc=pltpu.VMEM((8, hidden_units), F32),
        kx=pltpu.VMEM((parts, span, LANES), BF16),
        kxt=pltpu.VMEM((parts, LANES, span), BF16),
        vx=pltpu.VMEM((parts, span, LANES), BF16),
        vxt=pltpu.VMEM((parts, LANES, span), BF16),
        dk=pltpu.VMEM((parts, span, LANES), F32),
        dv=pltpu.VMEM((parts, span, LANES), F32),
        scores=pltpu.VMEM((parts, span, span), F32),
        raised=pltpu.VMEM((parts, span, span), BF16),
        att=pltpu.VMEM((LANES, span), F32),
        dq=pltpu.VMEM((LANES, span), F32),
        ga=pltpu.VMEM((LANES, span), BF16),
        gat=pltpu.VMEM((span, LANES), BF16),
        attt=pltpu.VMEM((width, span), BF16),
        gpt=pltpu.VMEM((merged, span), BF16),
        gp=pltpu.VMEM((span, merged), BF16),
        dkv_out=pltpu.VMEM((parts, span, LANES), BF16),
        dkv_in=pltpu.VMEM((parts, span, LANES), BF16),
        total=pltpu.VMEM((span, LANES), F32),
        grads=pltpu.VMEM(grads_shape, BF16),
        load_sem=pltpu.SemaphoreType.DMA((6,)),
        kv_sem=pltpu.SemaphoreType.DMA((2, parts)),
        dkv_sem=pltpu.SemaphoreType.DMA((2, parts)),
    )
    names = [*small, *large, *outs, *scratch]
    results = pl.pallas_call(
        functools.partial(layer_kernel, names, parts, inside),
        out_shape=[shape for shape, _ in outs.values()],
        in_specs=[vmem] * len(small) + [anywhere] * len(large),
        out_specs=[spec for _, spec in outs.values()],
        scratch_shapes=list(scratch.values()),
        compiler_params=pltpu.CompilerParams(
            collective_id=0, has_side_effects=True, vmem_limit_bytes=63 * 2**20
        ),
        name="layer",
    )(*small.values(), *large.values())
    outputs, input_grads, grads = results

    blocks = 8
    fc = grads[0:3].transpose(4, 1, 5, 0, 2, 3, 6).reshape(width, hidden_units)
    proj = grads[3:6].transpose(4, 1, 2, 3, 5, 0, 6).reshape(hidden_units, width)
    o = grads[6].transpose(3, 0, 4, 1, 2, 5).reshape(width, 4, BLOCK)[:, :, :192].reshape(width, width)
    qkv = grads[7].transpose(3, 0, 4, 1, 2, 5).reshape(width, 4 * BLOCK)
    lines = qkv[:, merged:].reshape(blocks, 96, LANES)
    vectors = [lines[:, 0, : merged // blocks], lines[:, 1:4]] + [lines[:, i, : width // blocks] for i in range(4, 9)]
    vectors = [vector.reshape(-1) for vector in vectors]
    every = [qkv[:, :merged], vectors[0], o, fc, vectors[1], proj, *vectors[2:]]
    shards = [lax.psum_scatter(item, "batch", scatter_dimension=0, tiled=True) for item in every]
    shards = [lax.psum(item, "seq").astype(F32) for item in shards]
    return (outputs[None], input_grads[None], *shards)


def solution(mesh):
    whole, part = P(), P("batch", "seq", None)
    in_specs = (part, P("batch", None), *[whole] * 11, part)
    matrix, vector = P("batch", None), P("batch")
    out_specs = (part, part, matrix, vector, matrix, matrix, vector, matrix, *[vector] * 5)
    return jax.shard_map(per_device, mesh=mesh, in_specs=in_specs, out_specs=out_specs, check_vma=False)
```

time: 582 us -> 385 us (0.66); the launches traced: 573 us -> 384 us
  waiting for transfers between devices: 312 us -> 152 us
  Pallas kernels: 0 us -> 108 us
  matrix products: 98.6 us -> 0 us
  other arithmetic: 52.8 us -> 7.75 us
  local copies, waits for them, and re-layouts: 40.1 us -> 63.9 us
  starting transfers between devices: 15.7 us -> 0.69 us
    pallas_call x0 -> x1, Pallas kernels: none -> 108 us  [per_device(): pl.pallas_call(functools.partial(layer_kernel, names, parts, inside), out...]
    dot_general x18 -> x0, matrix products: 98.6 us -> none  [the longest x1 18.7 us: per_device(): hidden = jnp.dot(second_in, w_fc, preferred_element_type=jnp.float32) + b_fc]
    ppermute x6 -> x0, waiting for transfers between devices: 91 us -> none  [from_behind(): return lax.ppermute(block, axis, route)]
    reduce_scatter x4 -> x3, waiting for transfers between devices: 213 us -> 131 us  [per_device(): lax.psum_scatter(item, 'batch', scatter_dimension=0, tiled=True)]
    transpose x0 -> x6, local copies, waits for them, and re-layouts: none -> 29 us  [the longest x2 15.8 us: per_device(): grads[3:6].transpose(4, 1, 2, 3, 5, 0, 6).reshape(hidden_units, width)]
    reduce_sum x5 -> x0, other arithmetic: 22.9 us -> none  [the longest x1 18.2 us: per_device(): jnp.sum(jnp.exp(stored[offset] - top[..., None]), axis=-1)]
    broadcast_in_dim x14 -> x0, local copies, waits for them, and re-layouts: 21.6 us -> none  [the longest x3 13.7 us: per_device(): jnp.full((rows_here, heads, span, span), -jnp.inf, jnp.float32)]
    reshape x0 -> x9, local copies, waits for them, and re-layouts: none -> 20.1 us  [the longest x1 11.3 us: per_device(): fc = grads[0:3].transpose(4, 1, 5, 0, 2, 3, 6).reshape(width, hidden_units)]
  transfers between devices with their start and end apart: 11 -> 5, of which waited for: 7 -> 4; matrix products, arithmetic and copies ran while one was open for 20% -> 13% of each run, Pallas kernels for 0% -> 0%
where the time goes in v1:
time: 385 us; the launch traced here: 384 us
  waiting for transfers between devices  152 us (39%)
  Pallas kernels  108 us (28%)
  local copies, waits for them, and re-layouts  63.9 us (17%)
  blocking collectives  35.8 us (9%)
  between operations  15.9 us (4%)
  other arithmetic  7.75 us (2%)
    reduce_scatter x3, waiting for transfers between devices, per_device(): lax.psum_scatter(item, 'batch', scatter_dimension=0, tiled=True)  131 us
    pallas_call x1, Pallas kernels, per_device(): pl.pallas_call(functools.partial(layer_kernel, names, parts, inside), out...  108 us
    unnamed x1, blocking collectives  26 us
    psum x1, waiting for transfers between devices, per_device(): shards = [lax.psum(item, 'seq').astype(F32) for item in shards]  20.7 us
    transpose x2, local copies, waits for them, and re-layouts, per_device(): grads[3:6].transpose(4, 1, 2, 3, 5, 0, 6).reshape(hidden_units, width)  15.8 us
    unnamed x26, local copies, waits for them, and re-layouts  11.4 us
    reshape x1, local copies, waits for them, and re-layouts, per_device(): fc = grads[0:3].transpose(4, 1, 5, 0, 2, 3, 6).reshape(width, hidden_units)  11.3 us
    psum x1, blocking collectives, per_device(): shards = [lax.psum(item, 'seq').astype(F32) for item in shards]  9.8 us
  transfers between devices with their start and end apart: 5, of which 4 were waited for; matrix products, arithmetic and copies ran while one was open for 13% of the time, Pallas kernels for 0%

profile of v1, /device:TPU:0, one launch (start us, length us, event | category | flops | bytes accessed | tf_op | source)
XLA Modules:
  0.0 384.1 jit_solution(10041127188802876329)
XLA Ops:
  7.2 0.0 reduce-scatter.13.cloned.1.call-start
  7.2 1.3 reshape.68.refs_1_
  8.5 1.3 reshape.70.refs_3_
  9.8 1.3 reshape.71.refs_4_
  11.0 1.3 reshape.72.refs_5_
  12.3 1.3 reshape.73.refs_6_
  13.6 1.3 reshape.74.refs_7_
  14.8 108.5 %layer.1 = (bf16[512,768]{1,0:T(8,128)(2,1)}, bf16[512,768]{1,0:T(8,128)(2,1)}, bf16[8,2,2,2,4,96,256]{6,5,4,3,2,1,0:T(8,128)(2,1)}) custom-call(s32[1,2048]{1,0:T(1,128)} %refs_0_.1, f32[1,896]{1,0:T(1,128)} %reshape.68.refs_1_, f32[1,3072]{1,0:T(1,128)} %bitcast.37, f32[1,768]{1,0:T(1,128)} %reshape.70.refs_3_, f32[1,768]{1,0:T(1,128)} %reshape.71.refs_4_, ...), custom_call_target="tpu_custom_call" | custom-call | tf_op jit(solution)/shard_map/layer/pallas_call | solution.py:443
  123.3 2.2 slice_bitcast_fusion.3
  125.5 0.1 copy.39
  125.6 1.5 copy.40
  127.1 2.4 copy.49
  129.4 0.0 reduce-scatter.13.cloned.1.call-update
  129.4 0.0 reduce-scatter.7.cloned.1.call-start
  129.5 1.6 copy.38
  131.1 1.1 reshape.75
  132.3 1.3 slice.56
  133.5 0.0 reduce-scatter.7.cloned.1.call-update
  133.5 0.3 reduce-scatter.11.cloned.1.call-start
  133.8 9.0 %slice_bitcast_fusion = (bf16[4,2,2,2,96,3,256]{6,4,0,3,2,1,5:T(8,128)(2,1)}, bf16[4,2,96,3,2,2,256]{6,2,0,5,4,1,3:T(8,128)(2,1)}) fusion(bf16[8,2,2,2,4,96,256]{6,5,4,3,2,1,0:T(8,128)(2,1)} %get-tuple-element.18), kind=kLoop, calls=%fused_computation | loop fusion | bytes 18874368 | tf_op jit(solution)/shard_map/transpose | solution.py:458
  142.8 6.7 %copy.42 = bf16[4,2,2,2,96,3,256]{6,5,4,3,2,1,0:T(4,128)(2,1)S(1)} copy(bf16[4,2,2,2,96,3,256]{6,4,0,3,2,1,5:T(8,128)(2,1)} %get-tuple-element.68) | data formatting | bytes 9437184 | tf_op jit(solution)/shard_map/transpose | solution.py:458
  149.6 3.5 copy.56
  153.1 0.0 reduce-scatter.11.cloned.1.call-update
  153.1 0.3 reduce-scatter.9.cloned.1.call-start
  153.4 9.4 %copy.41 = bf16[4,2,96,3,2,2,256]{6,5,4,3,2,1,0:T(2,128)(2,1)} copy(bf16[4,2,96,3,2,2,256]{6,2,0,5,4,1,3:T(8,128)(2,1)} %get-tuple-element.69) | data formatting | bytes 9437184 | tf_op jit(solution)/shard_map/transpose | solution.py:457
  162.8 11.3 %reshape.79 = bf16[768,3072]{1,0:T(8,128)(2,1)} reshape(bf16[4,2,96,3,2,2,256]{6,5,4,3,2,1,0:T(2,128)(2,1)} %copy.41) | data formatting | bytes 9437184 | tf_op jit(solution)/shard_map/reshape | solution.py:457
  174.1 0.0 all-reduce.12.cloned.1.call-start
  174.2 0.0 reduce-scatter.13.cloned.1.call-done
  174.2 1.7 copy.50
  176.0 19.8 %reduce-scatter.7.cloned.1.call-done = bf16[96,896]{1,0:T(8,128)(2,1)} async-done(((bf16[768,896]{1,0:T(8,128)(2,1)}), bf16[96,896]{1,0:T(8,128)(2,1)}) %reduce-scatter.7.cloned.1.call-update) | async-done | bytes 172048 | tf_op jit(solution)/shard_map/reduce_scatter | solution.py:465
  195.8 55.5 %reduce-scatter.11.cloned.1.call-done = bf16[384,768]{1,0:T(8,128)(2,1)} async-done(((bf16[3072,768]{1,0:T(8,128)(2,1)}), bf16[384,768]{1,0:T(8,128)(2,1)}) %reduce-scatter.11.cloned.1.call-update) | async-done | bytes 589840 | tf_op jit(solution)/shard_map/reduce_scatter | solution.py:465
  251.3 55.6 %reduce-scatter.9.cloned.1.call-done = bf16[96,3072]{1,0:T(8,128)(2,1)} async-done(((bf16[768,3072]{1,0:T(8,128)(2,1)}), bf16[96,3072]{1,0:T(8,128)(2,1)}) %reduce-scatter.9.cloned.1.call-update) | async-done | bytes 589840 | tf_op jit(solution)/shard_map/reduce_scatter | solution.py:465
  306.9 0.1 slice.57
  307.0 0.1 slice_reduce_fusion
  307.1 0.1 reshape_squeeze.19
  307.2 0.1 reshape_squeeze.20
  307.3 0.1 reshape_squeeze.21
  307.4 0.1 reshape_squeeze.22
  307.5 0.1 reshape_squeeze.23
  307.6 0.1 reshape_squeeze.18
  307.7 0.6 dynamic-slice
  308.9 26.0 %all-reduce.7 = (bf16[896]{0:T(1024)(128)(2,1)S(1)}, bf16[3072]{0:T(1024)(128)(2,1)S(1)}, bf16[768]{0:T(1024)(128)(2,1)S(1)}, bf16[768]{0:T(1024)(128)(2,1)S(1)}...) all-reduce(bf16[896]{0:T(1024)(128)(2,1)S(1)} %reshape_squeeze.18, ...), channel_id=3, replica_groups=mesh['seq'=4,'batch'=8] {'batch'}, use_global_device_ids=true, to_apply=%region_2.0.clone | all-reduce | flops 7808 | bytes 31232
  334.9 0.1 dynamic-slice.11
  335.0 0.1 dynamic-slice.13
  335.1 0.1 dynamic-slice.5
  335.1 0.1 dynamic-slice.7
  335.2 0.1 dynamic-slice.9
  336.6 0.1 dynamic-slice.3
  336.7 0.1 dynamic-slice.1
  336.7 9.8 %all-reduce.8 = (bf16[112]{0:T(256)(128)(2,1)S(1)}, bf16[384]{0:T(512)(128)(2,1)S(1)}, bf16[96]{0:T(256)(128)(2,1)S(1)}, bf16[96]{0:T(256)(128)(2,1)S(1)}, bf16[...) all-reduce(bf16[112]{0:T(256)(128)(2,1)S(1)} %dynamic-slice.1, ...), channel_id=1, replica_groups=mesh['seq'=4,'batch'=8] {'seq'}, use_global_device_ids=true, to_apply=%region_3.0 | all-reduce | flops 976 | bytes 3904 | tf_op jit(solution)/shard_map/psum | solution.py:466
  346.5 0.6 convert_element_type.37
  347.1 0.5 convert_element_type.34
  347.6 0.5 convert_element_type.39
  348.2 0.5 convert_element_type.40
  348.7 0.5 convert_element_type.41
  349.2 0.5 convert_element_type.42
  349.7 0.5 convert_element_type.43
  350.2 20.7 %all-reduce.12.cloned.1.call-done = (bf16[96,768]{0,1:T(8,128)(2,1)}, bf16[96,896]{1,0:T(8,128)(2,1)}, bf16[96,3072]{1,0:T(8,128)(2,1)}, bf16[384,768]{1,0:T(8,128)(2,1)}) async-done(((bf16[96,768]{0,1:T(8,128)(2,1)}, bf16[96,896]{1,0:T(8,128)(2,1)}, bf16[96,3072]{1,0:T(8,128)(2,1)}, bf16[384,768]{1,0:T(8,128)(2,1)}), (bf16[96,768]{0,1:T(8,128)(2,1)}, bf16[96,896]{1,0:T(8,128)(2,1)}, ...) | async-done | bytes 1499152 | tf_op jit(solution)/shard_map/psum | solution.py:466
  370.9 2.2 convert_element_type.36
  373.1 1.1 convert_element_type.38
  374.2 0.8 convert_element_type.33
  375.0 0.9 copy.48
  375.9 0.9 copy.63
  376.7 0.9 copy.64
  (17 shorter events, 0.1 us)
Async XLA Ops:
  7.2 167.0 %reduce-scatter.13.cloned.1.call-start = ((), (), s32[]{:S(2)}) async-start(), calls=%async_computation.7 | async-start | bytes 1327104
  129.4 66.4 %reduce-scatter.7.cloned.1.call-start = ((), (), s32[]{:S(2)}) async-start(), calls=%async_computation.4 | async-start | bytes 1548288 | tf_op jit(solution)/shard_map/reduce_scatter | solution.py:465
  133.5 117.8 %reduce-scatter.11.cloned.1.call-start = ((), (), s32[]{:S(2)}) async-start(), calls=%async_computation.6 | async-start | bytes 5308416 | tf_op jit(solution)/shard_map/reduce_scatter | solution.py:465
  153.1 153.8 %reduce-scatter.9.cloned.1.call-start = ((), (), s32[]{:S(2)}) async-start(), calls=%async_computation.5 | async-start | bytes 5308416 | tf_op jit(solution)/shard_map/reduce_scatter | solution.py:465
  174.1 133.5 %copy-start.5 = (u32[32]{0:T(128)S(1)}, u32[32]{0:T(128)}, u32[]{:S(2)}) copy-start(u32[32]{0:T(128)} %constant.5) | copy-start | bytes 388
  174.1 196.7 %all-reduce.12.cloned.1.call-start = ((), (), s32[]{:S(2)}) async-start(), calls=%async_computation.8 | async-start | bytes 3096576 | tf_op jit(solution)/shard_map/psum | solution.py:466
  370.9 2.3 copy-start.2
  370.9 3.4 copy-start.4
  373.1 1.9 copy-start.3
  373.1 2.7 copy-start.1
  374.2 2.5 copy-start
Sparse Core Ops, SparseCore 0:
  129.6 32.2 reduce-scatter.12
  164.1 31.6 reduce-scatter.6
  198.2 53.0 reduce-scatter.10
  253.6 53.3 reduce-scatter.8
  311.1 59.7 all-reduce.11

commit v2 on v1

--- a/solution.py
+++ b/solution.py
@@ -22,6 +22,24 @@
 BF16 = jnp.bfloat16
 
 CHUNKS = 8
+PIECE = 96
+SLOTS = 4
+
+
+def x_first(chunk):
+    return chunk % 2 == 0
+
+
+def place(chunk, b, quarter, inside):
+    y, x = quarter // 2, quarter % 2
+    p, s = (x, y) if inside and x_first(chunk) else (y, x)
+    return (((b % 2 * 2 + p) * 2 + s) * 4 + b // 2) * PIECE
+
+
+def chunk_ref(r, chunk):
+    if chunk < 6:
+        return r.grads.at[chunk]
+    return r.wp.at[:, (chunk - 6) * BLOCK : (chunk - 5) * BLOCK]
 
 
 def mm(a, b, ca=1, cb=0):
@@ -38,6 +56,25 @@
 
 def rows_of(shape):
     return lax.broadcasted_iota(jnp.int32, shape, 0)
+
+
+SCHEDULE = {
+    3: [("send_b", 0), ("send_a", 2)],
+    4: [("send_b", 1), ("send_a", 3)],
+    6: [("send_c", 0), ("send_c", 1)],
+    8: [("send_b", 2), ("send_a", 4)],
+    9: [("send_b", 3), ("send_a", 5)],
+    10: [("send_d", 0)],
+    11: [("send_d", 1), ("send_c", 2)],
+    12: [("send_c", 3)],
+    13: [("send_b", 4)],
+    14: [("send_b", 5)],
+    15: [("send_d", 2)],
+    16: [("send_d", 3), ("send_c", 4)],
+    17: [("send_c", 5)],
+    20: [("send_d", 4)],
+    21: [("send_d", 5)],
+}
 
 
 def gelu_parts(hidden):
@@ -71,11 +108,21 @@
         load.start()
 
     barrier = pltpu.get_barrier_semaphore()
-    for distance in range(1, parts):
-        pl.semaphore_signal(
-            barrier, inc=1, device_id=(lax.rem(mine + distance, parts), batch), device_id_type=MESH
-        )
-    pl.semaphore_wait(barrier, parts - 1)
+    peers = [(lax.rem(mine + distance, parts), batch) for distance in range(1, parts)]
+    summing = Summing(r, mine, batch, parts) if inside else None
+    if inside:
+        peers += [summing.core_peer, *summing.z_peers]
+    for peer in peers:
+        pl.semaphore_signal(barrier, inc=1, device_id=peer, device_id_type=MESH)
+    pl.semaphore_wait(barrier, len(peers))
+
+    def keep(chunk, b, quarter, value):
+        row = place(chunk, b, quarter, inside)
+        chunk_ref(r, chunk)[row : row + PIECE, :] = value.astype(BF16)
+
+    def step(*steps):
+        for kind, chunk in steps if inside else ():
+            getattr(summing, kind)(chunk)
 
     loads[0].wait()
 
@@ -90,8 +137,8 @@
     for i in range(span // LANES):
         normed, _ = norm_tile(i)
         rows = pl.ds(i * LANES, LANES)
-        first = normed * r.g1[...] + r.s1[...]
-        second = normed * r.g2[...] + r.s2[...]
+        first = normed * r.g1[...][None] + r.s1[...][None]
+        second = normed * r.g2[...][None] + r.s2[...][None]
         r.fi[rows, :] = first.astype(BF16)
         r.si[rows, :] = second.astype(BF16)
         r.fit[:, rows] = first.T.astype(BF16)
@@ -123,7 +170,7 @@
         return r.docs[0:1, pl.ds(pl.multiple_of(part * span, LANES), span)]
 
     loads[1].wait()
-    key_value = mm(r.fi[...], r.wq[:, width:]) + r.bq[:, width:]
+    key_value = mm(r.fi[...], r.wq[:, width:]) + r.bq[width:][None]
     low = lane < HEAD
     key_value = rotate(key_value, jnp.where(low, table_cos, 1.0), jnp.where(low, table_sin, 0.0))
     r.kv[0] = key_value.astype(BF16)
@@ -137,7 +184,7 @@
     query_feature = jnp.where(feature_row == docs_row(0), 1.0, 0.0).T
     for i in range(heads // 2):
         columns = slice(i * LANES, (i + 1) * LANES)
-        tile = mm(r.fi[...], r.wq[:, columns]) + r.bq[:, columns]
+        tile = mm(r.fi[...], r.wq[:, columns]) + r.bq[columns][None]
         tile = rotate(tile, table_cos, table_sin) * (LOG2E / math.sqrt(HEAD))
         r.q[2 * i] = jnp.where(low, tile, query_feature).astype(BF16)
         r.q[2 * i + 1] = jnp.where(low, pltpu.roll(tile, HEAD, 1), query_feature).astype(BF16)
@@ -155,34 +202,31 @@
     ones_rows = jnp.ones((8, span), BF16)
     group = 2 * 4 * 96
 
-    def feed_forward(g, _):
-        columns = pl.ds(pl.multiple_of(g * group, LANES), group)
-        hidden = mm(r.si[...], r.wfc[:, columns]) + r.bfc[:, columns]
+    for g in range(hidden_units // group):
+        columns = slice(g * group, (g + 1) * group)
+        hidden = mm(r.si[...], r.wfc[:, columns]) + r.bfc[columns][None]
         grad_act = mm(r.cot[...], r.wp[columns, :], 1, 1)
         below, slope = gelu_parts(hidden)
         r.act[...] = (hidden * below).astype(BF16)
         r.gh[...] = (grad_act * (below + slope)).astype(BF16)
         grad_w = mm(r.sit[...], r.gh[...])
         for k in range(group // BLOCK):
-            place = g * (group // BLOCK) + k
+            chunk, quarter = divmod(g * (group // BLOCK) + k, 4)
             for b in range(8):
-                r.grads[place // 4, b % 2, lax.rem(place, 4) // 2, lax.rem(place, 2), b // 2] = grad_w[
-                    b * 96 : (b + 1) * 96, k * BLOCK : (k + 1) * BLOCK
-                ].astype(BF16)
+                keep(chunk, b, quarter, grad_w[b * PIECE : (b + 1) * PIECE, k * BLOCK : (k + 1) * BLOCK])
+        step(*[("send", g - 1)] * (g > 0))
         grad_w = mm(r.act[...], r.cot[...], 0, 0)
         for k in range(3):
             for c in range(2):
                 for q in range(4):
-                    row = (c * 4 + q) * 96
-                    r.grads[3 + k, c, q // 2, q % 2, g] = grad_w[
-                        row : row + 96, k * BLOCK : (k + 1) * BLOCK
-                    ].astype(BF16)
+                    row = (c * 4 + q) * PIECE
+                    keep(3 + k, 2 * g + c, q, grad_w[row : row + PIECE, k * BLOCK : (k + 1) * BLOCK])
+        if g == 3:
+            step(("send", 3), ("send_a", 0), ("send_a", 1))
         r.sum_fc[:, columns] = mm(ones_rows, r.gh[...])
         r.result[...] += mm(r.act[...], r.wp[columns, :])
         r.second[...] += mm(r.gh[...], r.wfc[:, columns], 1, 1)
-        return 0
-
-    lax.fori_loop(0, hidden_units // group, feed_forward, 0)
+    step(("send", 4), ("send", 5))
 
     for distance in range(parts):
 
@@ -204,14 +248,24 @@
     r.dk[...] = jnp.zeros_like(r.dk)
     r.dv[...] = jnp.zeros_like(r.dv)
 
+    def scheduled(now):
+        for when, steps in SCHEDULE.items():
+
+            @pl.when(now == when)
+            def _():
+                step(*steps)
+
     def one_head(h, _):
         rows = pl.ds(pl.multiple_of(h * HEAD, HEAD), HEAD)
+
+        def columns_of(distance):
+            return pl.ds(pl.multiple_of(distance * span, LANES), span)
 
         def scores(distance, causal):
             raw = mm(r.kx[distance], r.q[h], 1, 1)
             if causal:
                 raw = jnp.where(rows_of(raw.shape) <= lanes_of(raw.shape), raw, FAR)
-            r.scores[distance] = raw
+            r.scores[:, columns_of(distance)] = raw
             return jnp.max(raw, axis=0, keepdims=True)
 
         top = scores(0, True)
@@ -219,12 +273,13 @@
         r.att[...] = jnp.zeros_like(r.att)
 
         def weigh(distance, _):
-            raised = jnp.exp2(r.scores[distance] - top).astype(BF16)
-            r.raised[distance] = raised
+            raised = jnp.exp2(r.scores[:, columns_of(distance)] - top).astype(BF16)
+            r.wfc[:span, columns_of(distance)] = raised
             r.att[...] += mm(r.vxt[distance], raised)
             return 0
 
         lax.fori_loop(0, mine + 1, weigh, 0)
+        scheduled(2 * h)
         inverse = 1.0 / r.att[HEAD : HEAD + 1, :]
         attended = r.att[:HEAD, :] * inverse
         r.attt[rows, :] = attended.astype(BF16)
@@ -240,7 +295,7 @@
 
         def back(distance, _):
             grad_probs = mm(r.vx[distance], r.ga[...])
-            raised = r.raised[distance]
+            raised = r.wfc[:span, columns_of(distance)]
             grad_scores = (raised.astype(F32) * grad_probs).astype(BF16)
             r.dv[distance] += mm(raised, r.gat[...])
             r.dk[distance] += mm(grad_scores, r.q[h])
@@ -249,6 +304,7 @@
 
         lax.fori_loop(0, mine + 1, back, 0)
         r.gpt[rows, :] = rotate_back(r, r.dq[:HEAD, :] * (1.0 / math.sqrt(HEAD))).astype(BF16)
+        scheduled(2 * h + 1)
         return 0
 
     lax.fori_loop(0, heads, one_head, 0)
@@ -268,7 +324,8 @@
         for q in range(4):
             piece = grad_w[b * 96 : (b + 1) * 96, q * 192 : (q + 1) * 192]
             piece = jnp.concatenate([piece, jnp.zeros((96, 64), F32)], axis=1)
-            r.grads[6, b % 2, q // 2, q % 2, b // 2] = piece.astype(BF16)
+            keep(6, b, q, piece)
+    step(("send", 6))
 
     r.total[...] = packed(0)
     for distance in range(1, parts):
@@ -288,24 +345,28 @@
             piece = grad_w[b * 96 : (b + 1) * 96, q * BLOCK : min((q + 1) * BLOCK, width + 2 * HEAD)]
             if q == 3:
                 piece = jnp.concatenate([piece, jnp.zeros((96, LANES), F32)], axis=1)
-            r.grads[7, b % 2, q // 2, q % 2, b // 2] = piece.astype(BF16)
-    for i in range((width + 2 * HEAD) // LANES):
+            keep(7, b, q, piece)
+    for i in range(width // LANES):
         columns = slice(i * LANES, (i + 1) * LANES)
-        r.gp[:, columns] = flip(r.gpt[columns, :]).astype(BF16)
-
-    r.first[...] = mm(r.gp[...], r.wq[...], 1, 1)
+        r.act[:, columns] = flip(r.gpt[columns, :]).astype(BF16)
+    r.gh[:, :LANES] = flip(r.gpt[width:, :]).astype(BF16)
+
+    first = mm(r.act[...], r.wq[:, :width], 1, 1) + mm(r.gh[:, :LANES], r.wq[:, width:], 1, 1)
+    for i in range(width // LANES):
+        (r.dk if i < parts else r.dv)[i % parts] = first[:, i * LANES : (i + 1) * LANES]
     sums = [jnp.zeros((1, width), F32) for _ in range(4)]
     for i in range(span // LANES):
         rows = pl.ds(i * LANES, LANES)
         normed, inverse_std = norm_tile(i)
-        first, second = r.first[rows, :], r.second[rows, :]
+        first = [(r.dk if j < parts else r.dv)[j % parts, rows, :] for j in range(width // LANES)]
+        first, second = jnp.concatenate(first, axis=1), r.second[rows, :]
         for j, term in enumerate((normed * first, first, normed * second, second)):
             sums[j] = sums[j] + jnp.sum(term, axis=0, keepdims=True)
-        scaled = first * r.g1[...] + second * r.g2[...]
+        scaled = first * r.g1[...][None] + second * r.g2[...][None]
         mean_one = jnp.mean(scaled, axis=-1, keepdims=True)
         mean_two = jnp.mean(scaled * normed, axis=-1, keepdims=True)
         back = inverse_std * (scaled - mean_one - normed * mean_two)
-        r.input_grads[rows, :] = (r.cot[rows, :].astype(F32) + back).astype(BF16)
+        r.si[rows, :] = (r.cot[rows, :].astype(F32) + back).astype(BF16)
 
     sum_qkv = mm(ones_rows, r.gpt[...], 1, 1)[0:1]
     sum_proj = mm(ones_rows, r.cot[...])[0:1]
@@ -314,16 +375,32 @@
         lines += [r.sum_fc[0:1, b * 384 + i * LANES : b * 384 + (i + 1) * LANES] for i in range(3)]
         lines += [cut(line, b * 96, 96) for line in (sum_proj, *sums)]
         lines.append(jnp.zeros((16 - len(lines), LANES), F32))
-        r.grads[7, b % 2, 1, 1, b // 2, 0:16, LANES:] = jnp.concatenate(lines, axis=0).astype(BF16)
+        row = place(7, b, 3, inside)
+        chunk_ref(r, 7)[row : row + 16, LANES:] = jnp.concatenate(lines, axis=0).astype(BF16)
+    step(("send", 7))
+    copies = [pltpu.make_async_copy(r.si, r.input_grads, r.load_sem.at[0])]
+    copies[0].start()
 
     for i in range(width // LANES):
         columns = slice(i * LANES, (i + 1) * LANES)
         r.fi[:, columns] = flip(r.attt[columns, :]).astype(BF16)
-    r.outputs[...] = (r.result[...] + r.x[...].astype(F32) + r.bp[...] + mm(r.fi[...], r.wo[...])).astype(BF16)
-
-    copy = pltpu.make_async_copy(r.grads, r.grads_out, r.load_sem.at[0])
-    copy.start()
-    copy.wait()
+    r.x[...] = (r.result[...] + r.x[...].astype(F32) + r.bp[...][None] + mm(r.fi[...], r.wo[...])).astype(BF16)
+    copies.append(pltpu.make_async_copy(r.x, r.outputs, r.load_sem.at[1]))
+    copies[1].start()
+
+    if inside:
+        step(("send_a", 6), ("send_a", 7))
+        step(*[("finish", k) for k in range(6)])
+        step(("send_b", 6), ("send_b", 7), ("send_c", 6), ("send_c", 7), ("send_d", 6), ("send_d", 7))
+        step(("finish", 6), ("finish", 7))
+        summing.close()
+    else:
+        copies.append(pltpu.make_async_copy(r.grads, r.grads_out.at[:6], r.load_sem.at[2]))
+        copies += [pltpu.make_async_copy(chunk_ref(r, k), r.grads_out.at[k], r.load_sem.at[k - 3]) for k in (6, 7)]
+        for copy in copies[2:]:
+            copy.start()
+    for copy in copies:
+        copy.wait()
     for distance in range(1, parts):
 
         @pl.when(mine + distance < parts)
@@ -350,6 +427,161 @@
     one, two = grads[:half], grads[half:ROT]
     cosine, sine = r.cos[...], r.sin[...]
     return jnp.concatenate([one * cosine + two * sine, two * cosine - one * sine, grads[ROT:]], axis=0)
+
+
+class Summing:
+    def __init__(self, r, mine, batch, parts):
+        self.r, self.mine, self.batch, self.parts = r, mine, batch, parts
+        y, x = mine // 2, lax.rem(mine, 2)
+        self.z, self.core = batch // 2, lax.rem(batch, 2)
+        self.axes = {"x": (x, (y * 2 + 1 - x, batch)), "y": (y, ((1 - y) * 2 + x, batch))}
+        self.core_peer = (mine, self.z * 2 + 1 - self.core)
+        self.z_peers = [(mine, lax.rem(self.z + i, 4) * 2 + self.core) for i in (1, 2, 3)]
+        self.seq_peers = [(lax.rem(mine + i, parts), batch) for i in range(1, parts)]
+        self.out_copies = []
+
+    def of(self, chunk):
+        first, then = ("x", "y") if x_first(chunk) else ("y", "x")
+        return *self.axes[first], *self.axes[then]
+
+    def copy(self, name, index, src, dst, peer):
+        sem = getattr(self.r, name + "_sem")
+        return pltpu.make_async_remote_copy(
+            src_ref=src,
+            dst_ref=dst,
+            send_sem=sem.at[0, index],
+            recv_sem=sem.at[1, index],
+            device_id=peer,
+            device_id_type=MESH,
+        )
+
+    def rows(self, chunk, start, count):
+        return chunk_ref(self.r, chunk).at[pl.ds(pl.multiple_of(start, PIECE), count)]
+
+    def pair(self, chunk):
+        src = self.rows(chunk, (1 - self.core) * 16 * PIECE, 16 * PIECE)
+        return self.copy("pair", chunk, src, self.r.pair.at[chunk % SLOTS], self.core_peer)
+
+    def half(self, chunk):
+        p, peer, _, _ = self.of(chunk)
+        src = self.rows(chunk, (self.core * 2 + 1 - p) * 8 * PIECE, 8 * PIECE)
+        return self.copy("half", chunk, src, self.r.half.at[chunk], peer)
+
+    def quarter(self, chunk):
+        p, _, s, peer = self.of(chunk)
+        src = self.rows(chunk, ((self.core * 2 + p) * 2 + 1 - s) * 4 * PIECE, 4 * PIECE)
+        return self.copy("quarter", chunk, src, self.r.quarter.at[chunk], peer)
+
+    def start_of_mine(self, chunk):
+        p, _, s, _ = self.of(chunk)
+        return ((self.core * 2 + p) * 2 + s) * 4 * PIECE
+
+    def line(self, chunk, i):
+        src = self.rows(chunk, self.start_of_mine(chunk) + lax.rem(self.z + i, 4) * PIECE, PIECE)
+        return self.copy("line", chunk * 3 + i - 1, src, self.r.line.at[chunk * 3 + i - 1], self.z_peers[i - 1])
+
+    def share(self, chunk, i):
+        here = self.r.share.at[chunk, self.mine]
+        return self.copy("share", chunk * 3 + i - 1, here, here, self.seq_peers[i - 1])
+
+    def add(self, chunk, start, other, other_start, pieces):
+        ref = chunk_ref(self.r, chunk)
+
+        def one(i, _):
+            to = pl.ds(pl.multiple_of(start + i * PIECE, PIECE), PIECE)
+            ref[to, :] += other[pl.ds(pl.multiple_of(other_start + i * PIECE, PIECE), PIECE), :]
+            return 0
+
+        lax.fori_loop(0, pieces, one, 0)
+
+    def send(self, chunk):
+        if chunk >= SLOTS:
+            pl.semaphore_wait(self.r.free_sem, 1)
+        self.pair(chunk).start()
+
+    def send_a(self, chunk):
+        self.pair(chunk).wait_recv()
+        p = self.of(chunk)[0]
+        got = self.r.pair.at[chunk % SLOTS]
+        for side in (1 - p, p):
+            self.add(chunk, (self.core * 2 + side) * 8 * PIECE, got, side * 8 * PIECE, 8)
+            if side is not p:
+                self.half(chunk).start()
+        if chunk + SLOTS < CHUNKS:
+            pl.semaphore_signal(self.r.free_sem, inc=1, device_id=self.core_peer, device_id_type=MESH)
+
+    def send_b(self, chunk):
+        self.half(chunk).wait_recv()
+        p, _, s, _ = self.of(chunk)
+        for side in (1 - s, s):
+            start = ((self.core * 2 + p) * 2 + side) * 4 * PIECE
+            self.add(chunk, start, self.r.half.at[chunk], side * 4 * PIECE, 4)
+            if side is not s:
+                self.quarter(chunk).start()
+
+    def send_c(self, chunk):
+        self.quarter(chunk).wait_recv()
+        start = self.start_of_mine(chunk)
+        for i in (1, 2, 3, 0):
+            z = lax.rem(self.z + i, 4) * PIECE
+            self.add(chunk, start + z, self.r.quarter.at[chunk], z, 1)
+            if i:
+                self.line(chunk, i).start()
+
+    def send_d(self, chunk):
+        total = self.rows(chunk, self.start_of_mine(chunk) + self.z * PIECE, PIECE)[...].astype(F32)
+        for i in (1, 2, 3):
+            self.line(chunk, i).wait_recv()
+            total = total + self.r.line[chunk * 3 + i - 1].astype(F32)
+        self.r.share[chunk, self.mine] = total.astype(BF16)
+        for i in (1, 2, 3):
+            self.share(chunk, i).start()
+
+    def finish(self, chunk):
+        r = self.r
+        for i in (1, 2, 3):
+            self.share(chunk, i).wait_recv()
+        quarters = [r.share[chunk, q].astype(F32) for q in range(4)]
+        top = chunk % 4 * LANES
+        left = chunk // 4 * 4 * BLOCK
+        if chunk == 6:
+            whole = jnp.concatenate([quarter[:, :192] for quarter in quarters], axis=1)
+        else:
+            whole = jnp.concatenate(quarters, axis=1)
+        r.scores[top : top + PIECE, left : left + whole.shape[1]] = whole
+        stage = lambda a, b: r.scores.at[top : top + PIECE, left + a : left + b]
+        if chunk < 3:
+            moves = [(stage(0, 1024), r.grad_fc.at[:, chunk * 1024 : (chunk + 1) * 1024])]
+        elif chunk < 6:
+            columns = slice((chunk - 3) * BLOCK, (chunk - 2) * BLOCK)
+            moves = [
+                (stage(q * BLOCK, (q + 1) * BLOCK), r.grad_proj.at[q * PIECE : (q + 1) * PIECE, columns])
+                for q in range(4)
+            ]
+        elif chunk == 6:
+            moves = [(stage(0, r.grad_o.shape[1]), r.grad_o)]
+        else:
+            moves = [(stage(0, r.grad_qkv.shape[1]), r.grad_qkv)]
+            lines = quarters[3][:16, LANES:]
+            r.grad_bq[...] = lines[0, : r.grad_bq.shape[0]]
+            for i in range(3):
+                r.grad_bfc[i * LANES : (i + 1) * LANES] = lines[1 + i]
+            for i, out in enumerate((r.grad_bp, r.grad_g1, r.grad_s1, r.grad_g2, r.grad_s2)):
+                out[...] = lines[4 + i, : out.shape[0]]
+        for src, dst in moves:
+            copy = pltpu.make_async_copy(src, dst, r.out_sem.at[len(self.out_copies)])
+            copy.start()
+            self.out_copies.append(copy)
+
+    def close(self):
+        for copy in self.out_copies:
+            copy.wait()
+        for chunk in range(CHUNKS):
+            for copy in (self.pair(chunk), self.half(chunk), self.quarter(chunk)):
+                copy.wait_send()
+            for i in (1, 2, 3):
+                self.line(chunk, i).wait_send()
+                self.share(chunk, i).wait_send()
 
 
 def kv_copy(r, mine, batch, parts, distance):
@@ -381,19 +613,29 @@
     heads = width // HEAD
     hidden_units = w_fc.shape[1]
     merged = width + 2 * HEAD
-    inside = False
+    inside = parts == 4 and lax.axis_size("batch") == 8
     vmem = pl.BlockSpec(memory_space=pltpu.VMEM)
     anywhere = pl.BlockSpec(memory_space=pl.ANY)
 
     small = dict(docs=doc_ids, bq=b_qkv, bfc=b_fc, bp=b_proj, g1=gain_one, s1=shift_one, g2=gain_two, s2=shift_two)
-    small = {name: value.reshape(1, -1) for name, value in small.items()}
     large = dict(x_h=inputs[0], cot_h=cotangent[0], wq_h=w_qkv, wo_h=w_o, wfc_h=w_fc, wp_h=w_proj)
-    grads_shape = (CHUNKS, 2, 2, 2, 4, 96, BLOCK)
-    outs = dict(
-        outputs=(jax.ShapeDtypeStruct((span, width), BF16), vmem),
-        input_grads=(jax.ShapeDtypeStruct((span, width), BF16), vmem),
-        grads_out=(jax.ShapeDtypeStruct(grads_shape, BF16), anywhere),
-    )
+    outs = dict(outputs=((span, width), BF16, anywhere), input_grads=((span, width), BF16, anywhere))
+    if inside:
+        outs |= dict(
+            grad_qkv=((width // 8, merged), F32, anywhere),
+            grad_bq=((merged // 8,), F32, vmem),
+            grad_o=((width // 8, width), F32, anywhere),
+            grad_fc=((width // 8, hidden_units), F32, anywhere),
+            grad_bfc=((hidden_units // 8,), F32, vmem),
+            grad_proj=((hidden_units // 8, width), F32, anywhere),
+            grad_bp=((width // 8,), F32, vmem),
+            grad_g1=((width // 8,), F32, vmem),
+            grad_s1=((width // 8,), F32, vmem),
+            grad_g2=((width // 8,), F32, vmem),
+            grad_s2=((width // 8,), F32, vmem),
+        )
+    else:
+        outs |= dict(grads_out=((CHUNKS, 32 * PIECE, BLOCK), BF16, anywhere))
     scratch = dict(
         x=pltpu.VMEM((span, width), BF16),
         cot=pltpu.VMEM((span, width), BF16),
@@ -414,7 +656,6 @@
         gh=pltpu.VMEM((span, width), BF16),
         result=pltpu.VMEM((span, width), F32),
         second=pltpu.VMEM((span, width), F32),
-        first=pltpu.VMEM((span, width), F32),
         sum_fc=pltpu.VMEM((8, hidden_units), F32),
         kx=pltpu.VMEM((parts, span, LANES), BF16),
         kxt=pltpu.VMEM((parts, LANES, span), BF16),
@@ -422,37 +663,53 @@
         vxt=pltpu.VMEM((parts, LANES, span), BF16),
         dk=pltpu.VMEM((parts, span, LANES), F32),
         dv=pltpu.VMEM((parts, span, LANES), F32),
-        scores=pltpu.VMEM((parts, span, span), F32),
-        raised=pltpu.VMEM((parts, span, span), BF16),
+        scores=pltpu.VMEM((span, parts * span), F32),
         att=pltpu.VMEM((LANES, span), F32),
         dq=pltpu.VMEM((LANES, span), F32),
         ga=pltpu.VMEM((LANES, span), BF16),
         gat=pltpu.VMEM((span, LANES), BF16),
         attt=pltpu.VMEM((width, span), BF16),
         gpt=pltpu.VMEM((merged, span), BF16),
-        gp=pltpu.VMEM((span, merged), BF16),
         dkv_out=pltpu.VMEM((parts, span, LANES), BF16),
         dkv_in=pltpu.VMEM((parts, span, LANES), BF16),
         total=pltpu.VMEM((span, LANES), F32),
-        grads=pltpu.VMEM(grads_shape, BF16),
+        grads=pltpu.VMEM((6, 32 * PIECE, BLOCK), BF16),
         load_sem=pltpu.SemaphoreType.DMA((6,)),
         kv_sem=pltpu.SemaphoreType.DMA((2, parts)),
         dkv_sem=pltpu.SemaphoreType.DMA((2, parts)),
     )
+    if inside:
+        scratch |= dict(
+            pair=pltpu.VMEM((SLOTS, 16 * PIECE, BLOCK), BF16),
+            half=pltpu.VMEM((CHUNKS, 8 * PIECE, BLOCK), BF16),
+            quarter=pltpu.VMEM((CHUNKS, 4 * PIECE, BLOCK), BF16),
+            line=pltpu.VMEM((CHUNKS * 3, PIECE, BLOCK), BF16),
+            share=pltpu.VMEM((CHUNKS, 4, PIECE, BLOCK), BF16),
+            pair_sem=pltpu.SemaphoreType.DMA((2, CHUNKS)),
+            half_sem=pltpu.SemaphoreType.DMA((2, CHUNKS)),
+            quarter_sem=pltpu.SemaphoreType.DMA((2, CHUNKS)),
+            line_sem=pltpu.SemaphoreType.DMA((2, CHUNKS * 3)),
+            share_sem=pltpu.SemaphoreType.DMA((2, CHUNKS * 3)),
+            out_sem=pltpu.SemaphoreType.DMA((17,)),
+            free_sem=pltpu.SemaphoreType.REGULAR,
+        )
     names = [*small, *large, *outs, *scratch]
     results = pl.pallas_call(
         functools.partial(layer_kernel, names, parts, inside),
-        out_shape=[shape for shape, _ in outs.values()],
+        out_shape=[jax.ShapeDtypeStruct(shape, dtype) for shape, dtype, _ in outs.values()],
         in_specs=[vmem] * len(small) + [anywhere] * len(large),
-        out_specs=[spec for _, spec in outs.values()],
+        out_specs=[spec for _, _, spec in outs.values()],
         scratch_shapes=list(scratch.values()),
         compiler_params=pltpu.CompilerParams(
             collective_id=0, has_side_effects=True, vmem_limit_bytes=63 * 2**20
         ),
         name="layer",
     )(*small.values(), *large.values())
-    outputs, input_grads, grads = results
-
+    outputs, input_grads, *shards = results
+    if inside:
+        return (outputs[None], input_grads[None], *shards)
+
+    grads = shards[0].reshape(CHUNKS, 2, 2, 2, 4, PIECE, BLOCK)
     blocks = 8
     fc = grads[0:3].transpose(4, 1, 5, 0, 2, 3, 6).reshape(width, hidden_units)
     proj = grads[3:6].transpose(4, 1, 2, 3, 5, 0, 6).reshape(hidden_units, width)

time: 385 us -> 161 us (0.42)
  waiting for transfers between devices: 152 us -> 0 us
  local copies, waits for them, and re-layouts: 63.9 us -> 10.5 us
  Pallas kernels: 108 us -> 149 us
  blocking collectives: 35.8 us -> 0 us
  between operations: 15.9 us -> 0.71 us
  other arithmetic: 7.75 us -> 0 us
    reduce_scatter x3 -> x0, waiting for transfers between devices: 131 us -> none  [per_device(): lax.psum_scatter(item, 'batch', scatter_dimension=0, tiled=True)]
    pallas_call x1, Pallas kernels: 108 us -> 149 us  [per_device(): pl.pallas_call(functools.partial(layer_kernel, names, parts, inside), out...]
    transpose x6 -> x0, local copies, waits for them, and re-layouts: 29 us -> none  [the longest x2 15.8 us: per_device(): grads[3:6].transpose(4, 1, 2, 3, 5, 0, 6).reshape(hidden_units, width)]
    unnamed x1 -> x0, blocking collectives: 26 us -> none
    psum x1 -> x0, waiting for transfers between devices: 20.7 us -> none  [per_device(): shards = [lax.psum(item, 'seq').astype(F32) for item in shards]]
    reshape x9 -> x0, local copies, waits for them, and re-layouts: 20.1 us -> none  [the longest x1 11.3 us: per_device(): fc = grads[0:3].transpose(4, 1, 5, 0, 2, 3, 6).reshape(width, hidden_units)]
    psum x1 -> x0, blocking collectives: 9.8 us -> none  [per_device(): shards = [lax.psum(item, 'seq').astype(F32) for item in shards]]
    convert_element_type x10 -> x0, other arithmetic: 7.75 us -> none  [per_device(): shards = [lax.psum(item, 'seq').astype(F32) for item in shards]]
  transfers between devices with their start and end apart: 5 -> 0, of which waited for: 4 -> 0; matrix products, arithmetic and copies ran while one was open for 13% -> 0% of each run, Pallas kernels for 0% -> 0%
where the time goes in v2:
time: 161 us; the launch traced here: 160 us
  Pallas kernels  149 us (93%)
  local copies, waits for them, and re-layouts  10.5 us (7%)
    pallas_call x1, Pallas kernels, per_device(): pl.pallas_call(functools.partial(layer_kernel, names, parts, inside), out...  149 us
    unnamed x37, local copies, waits for them, and re-layouts  10.5 us

profile of v2, /device:TPU:0, one launch (start us, length us, event | category | flops | bytes accessed | tf_op | source)
XLA Modules:
  0.0 160.3 jit_solution(15304577724584580016)
XLA Ops:
  0.7 149.1 %layer.1 = (bf16[512,768]{1,0:T(8,128)(2,1)}, bf16[512,768]{1,0:T(8,128)(2,1)}, f32[96,896]{1,0:T(8,128)}, f32[112]{0:T(128)}, f32[96,768]{1,0:T(8,128)}, /*inde...) custom-call(s32[1,2048]{1,0:T(1,128)} %refs_0_.1, ...), custom_call_target="tpu_custom_call" | custom-call | tf_op jit(solution)/shard_map/layer/pallas_call | solution.py:697
  149.7 0.0 copy-start.2
  149.8 2.1 %copy.40 = bf16[1,512,768]{2,1,0:T(8,128)(2,1)} copy(bf16[1,512,768]{2,1,0:T(8,128)(2,1)} %bitcast.5) | data formatting | bytes 1572864
  151.9 0.0 copy-done.2
  151.9 0.0 copy-start.3
  151.9 0.0 copy-start.11
  151.9 0.0 copy-start.4
  151.9 0.0 copy-start.1
  151.9 0.9 copy.41
  152.8 0.2 copy-done.3
  153.0 0.7 copy.42
  153.8 0.0 copy-done.11
  153.8 0.5 copy.43
  154.3 0.0 copy-done.4
  154.3 0.7 copy.44
  155.0 0.0 copy-done.1
  155.0 0.0 copy-start.5
  155.0 0.0 copy-start
  155.0 1.0 copy.45
  156.0 0.0 copy-done.5
  156.0 0.6 copy.46
  156.6 0.1 copy-done
  156.7 0.0 copy-start.10
  156.7 0.0 copy-start.9
  156.7 0.0 copy-start.8
  156.7 0.0 copy-start.7
  156.7 0.0 copy-start.6
  156.7 1.0 copy.47
  157.7 0.0 copy-done.10
  157.7 0.5 copy.48
  158.3 0.0 copy-done.9
  158.3 0.5 copy.49
  158.8 0.0 copy-done.8
  158.8 0.5 copy.50
  159.3 0.0 copy-done.7
  159.3 0.5 copy.51
  159.8 0.0 copy-done.6
  159.8 0.5 copy.52
Async XLA Ops:
  149.7 2.1 %copy-start.2 = (bf16[512,768]{1,0:T(8,128)(2,1)S(1)}, bf16[512,768]{1,0:T(8,128)(2,1)}, u32[]{:S(2)}) copy-start(bf16[512,768]{1,0:T(8,128)(2,1)} %get-tuple-element.27) | copy-start | bytes 2359300
  151.9 1.1 copy-start.3
  151.9 1.9 %copy-start.11 = (f32[112]{0:T(128)S(1)}, f32[112]{0:T(128)}, u32[]{:S(2)}) copy-start(f32[112]{0:T(128)} %get-tuple-element.55) | copy-start | bytes 1348
  151.9 2.4 %copy-start.4 = (f32[96,768]{1,0:T(8,128)S(1)}, f32[96,768]{1,0:T(8,128)}, u32[]{:S(2)}) copy-start(f32[96,768]{1,0:T(8,128)} %get-tuple-element.56) | copy-start | bytes 884740
  151.9 3.1 %copy-start.1 = (f32[96,3072]{1,0:T(8,128)S(1)}, f32[96,3072]{1,0:T(8,128)}, u32[]{:S(2)}) copy-start(f32[96,3072]{1,0:T(8,128)} %get-tuple-element.57) | copy-start | bytes 3538948
  155.0 1.0 copy-start.5
  155.0 1.7 %copy-start = (f32[384,768]{1,0:T(8,128)S(1)}, f32[384,768]{1,0:T(8,128)}, u32[]{:S(2)}) copy-start(f32[384,768]{1,0:T(8,128)} %get-tuple-element.59) | copy-start | bytes 3538948
  156.7 1.0 copy-start.10
  156.7 1.6 copy-start.9
  156.7 2.1 %copy-start.8 = (f32[96]{0:T(128)S(1)}, f32[96]{0:T(128)}, u32[]{:S(2)}) copy-start(f32[96]{0:T(128)} %get-tuple-element.62) | copy-start | bytes 1156
  156.7 2.6 %copy-start.7 = (f32[96]{0:T(128)S(1)}, f32[96]{0:T(128)}, u32[]{:S(2)}) copy-start(f32[96]{0:T(128)} %get-tuple-element.63) | copy-start | bytes 1156
  156.7 3.1 %copy-start.6 = (f32[96]{0:T(128)S(1)}, f32[96]{0:T(128)}, u32[]{:S(2)}) copy-start(f32[96]{0:T(128)} %get-tuple-element.64) | copy-start | bytes 1156
